TPU v7x, 256 devices: a whole 4x4x8 slice. The times are simulated.
256 devices in a mesh: gx: 16 (over x, y_lo, core), gy: 16 (over y_hi, z).
Axes of the slice: x: 4, y: 4 (y_hi: 2, y_lo: 2; y = y_hi * 2 + y_lo), z: 8, core: 2. Of those that a mesh axis runs over, the one named last changes fastest.
Arguments:
- particles: bfloat16 [64, 64, 16, 128], P('gx', 'gy'), may hold values from -6 to 6
- neighbours: int32 [64, 64, 16, 16], P('gx', 'gy'), may hold values from 0 to 143
- edge_valid: int32 [64, 64, 16, 16], P('gx', 'gy'), may hold values 0 or 1
- dropout_keep: int32 [2, 2, 64, 64, 16, 128], P(None, None, 'gx', 'gy'), may hold values 0 or 1
- weights: bfloat16 [2, 7, 128, 128], replicated, may hold values from -0.5 to 0.5
- biases: float32 [2, 3, 128], replicated, may hold values from -3 to 3
- cotangent: float32 [64, 64, 16, 128], P('gx', 'gy'), may hold values from -12 to 12
Outputs:
- particle_grad: float32 [64, 64, 16, 128], P('gx', 'gy')
- weight_grad: float32 [2, 7, 128, 128], replicated
- bias_grad: float32 [2, 3, 128], replicated
All inputs are finite; a program needn't handle non-finite values. No bound on the sum of `edge_valid` or of `dropout_keep` on one device may be relied on, other than what follows from the above.
Results may differ from a plain program's by a relative error of at most 0.011.
Values may be sent and summed in bfloat16 or wider, within the bound.
A program may use at most 64 MiB of HBM per device.

v0:
```python
import jax
import jax.numpy as jnp
from jax import lax
from jax.sharding import PartitionSpec as P

keep_scale = 10.0 / 9.0


def padded(cells, sides, width):
    for axis, dim in sides:
        count = lax.axis_size(axis)
        head = lax.slice_in_dim(cells, 0, width, axis=dim)
        tail = lax.slice_in_dim(cells, cells.shape[dim] - width, cells.shape[dim], axis=dim)
        cells = jnp.concatenate(
            [
                lax.ppermute(tail, axis, [(i, (i + 1) % count) for i in range(count)]),
                cells,
                lax.ppermute(head, axis, [((i + 1) % count, i) for i in range(count)]),
            ],
            axis=dim,
        )
    return cells


def shifted(block, axis, distance):
    devices = range(lax.axis_size(axis))
    route = [((i - distance) % len(devices), i) for i in devices]
    return lax.ppermute(block, axis, route)


def silu_grad(in_value):
    sigmoid_val = jax.nn.sigmoid(in_value)
    return sigmoid_val * (1.0 + in_value * (1.0 - sigmoid_val))


def back_dot(left_op, right_op):
    return lax.dot_general(
        left_op, right_op, (((0,), (0,)), ((), ())), preferred_element_type=jnp.float32
    )


def side_dot(left_op, right_op):
    return lax.dot_general(
        left_op, right_op, (((1,), (1,)), ((), ())), preferred_element_type=jnp.float32
    )


def edge_forward(near_proj, far_table, row_index, valid_rows, mid_w, mid_b):
    node_count, feat_width = near_proj.shape
    slot_k = row_index.shape[1]
    fetched = jnp.take(far_table, row_index.reshape(-1), axis=0).reshape(
        node_count, slot_k, feat_width
    )
    pre_one = near_proj[:, None, :] + fetched.astype(jnp.float32)
    edge_first = jax.nn.silu(pre_one).astype(jnp.bfloat16).reshape(-1, feat_width)
    pre_two = jnp.dot(edge_first, mid_w, preferred_element_type=jnp.float32) + mid_b
    edge_second = jax.nn.silu(pre_two).astype(jnp.bfloat16).reshape(node_count, slot_k, feat_width)
    return jnp.einsum(
        "qk,qkh->qh",
        valid_rows.astype(jnp.bfloat16),
        edge_second,
        preferred_element_type=jnp.float32,
    )


def edge_backward(near_proj, far_table, row_index, valid_rows, mid_w, mid_b, d_pooled):
    node_count, feat_width = near_proj.shape
    slot_k = row_index.shape[1]
    fetched = jnp.take(far_table, row_index.reshape(-1), axis=0).reshape(
        node_count, slot_k, feat_width
    )
    pre_one = near_proj[:, None, :] + fetched.astype(jnp.float32)
    edge_first = jax.nn.silu(pre_one).astype(jnp.bfloat16).reshape(-1, feat_width)
    pre_two = jnp.dot(edge_first, mid_w, preferred_element_type=jnp.float32) + mid_b
    lifted = valid_rows.astype(jnp.float32)[:, :, None] * d_pooled.astype(jnp.float32)[:, None, :]
    d_two = lifted.reshape(-1, feat_width) * silu_grad(pre_two)
    d_two_b = d_two.astype(jnp.bfloat16)
    grad_mid_w = back_dot(edge_first, d_two_b)
    d_first = side_dot(d_two_b, mid_w).reshape(node_count, slot_k, feat_width)
    d_one = d_first * silu_grad(pre_one)
    return (
        jnp.sum(d_one, axis=1),
        d_one,
        grad_mid_w,
        jnp.sum(d_two, axis=0),
        jnp.sum(d_one, axis=(0, 1)),
    )


def spread_far(far_own):
    return padded(far_own, (("gx", 0), ("gy", 1)), 1)


def fold_axis_x(buffer):
    inner = buffer.shape[0] - 2
    from_above = shifted(buffer[0].astype(jnp.bfloat16), "gx", -1).astype(jnp.float32)
    from_below = shifted(buffer[inner + 1].astype(jnp.bfloat16), "gx", 1).astype(jnp.float32)
    middle = buffer[1 : inner + 1]
    middle = middle.at[inner - 1].add(from_above)
    return middle.at[0].add(from_below)


def fold_axis_y(buffer):
    inner = buffer.shape[1] - 2
    from_above = shifted(buffer[:, 0].astype(jnp.bfloat16), "gy", -1).astype(jnp.float32)
    from_below = shifted(buffer[:, inner + 1].astype(jnp.bfloat16), "gy", 1).astype(jnp.float32)
    middle = buffer[:, 1 : inner + 1]
    middle = middle.at[:, inner - 1].add(from_above)
    return middle.at[:, 0].add(from_below)


def fold_back(buffer):
    return fold_axis_y(fold_axis_x(buffer))


def shards(particles, neighbours, edge_valid, dropout_keep, weights, biases, cotangent):
    span_x, span_y, slots, feat_width = particles.shape
    slot_k = neighbours.shape[3]
    layer_count = weights.shape[0]
    node_count = span_x * span_y * slots
    offset_code = neighbours // slots
    within_col = neighbours % slots
    cell_x = lax.broadcasted_iota(jnp.int32, neighbours.shape, 0)
    cell_y = lax.broadcasted_iota(jnp.int32, neighbours.shape, 1)
    target_x = cell_x + offset_code // 3
    target_y = cell_y + offset_code % 3
    row_index = ((target_x * (span_y + 2) + target_y) * slots + within_col).reshape(
        node_count, slot_k
    )
    valid_rows = edge_valid.reshape(node_count, slot_k)
    state = particles.reshape(node_count, feat_width)
    saved = []
    for layer_no in range(layer_count):
        layer_w = weights[layer_no]
        layer_b = biases[layer_no]
        keep_msg = (
            dropout_keep[layer_no, 0].reshape(node_count, feat_width).astype(jnp.float32)
            * keep_scale
        )
        keep_node = (
            dropout_keep[layer_no, 1].reshape(node_count, feat_width).astype(jnp.float32)
            * keep_scale
        )
        near_proj = jnp.dot(state, layer_w[0], preferred_element_type=jnp.float32) + layer_b[0]
        far_own = jnp.dot(state, layer_w[1], preferred_element_type=jnp.float32).astype(
            jnp.bfloat16
        )
        far_table = spread_far(far_own.reshape(span_x, span_y, slots, feat_width)).reshape(
            -1, feat_width
        )
        pooled = edge_forward(
            near_proj, far_table, row_index, valid_rows, layer_w[4], layer_b[1]
        ).astype(jnp.bfloat16)
        message = (
            jnp.dot(pooled, layer_w[5], preferred_element_type=jnp.float32) * keep_msg / slot_k
        ).astype(jnp.bfloat16)
        node_pre = (
            jnp.dot(state, layer_w[2], preferred_element_type=jnp.float32)
            + jnp.dot(message, layer_w[3], preferred_element_type=jnp.float32)
            + layer_b[2]
        )
        node_hidden = (jax.nn.silu(node_pre) * keep_node).astype(jnp.bfloat16)
        saved.append(
            (
                state,
                near_proj,
                far_table,
                pooled,
                message,
                node_pre,
                node_hidden,
                keep_msg,
                keep_node,
            )
        )
        state = (
            state.astype(jnp.float32)
            + jnp.dot(node_hidden, layer_w[6], preferred_element_type=jnp.float32)
        ).astype(jnp.bfloat16)
    norm_scale = 1.0 / (node_count * lax.axis_size("gx") * lax.axis_size("gy")) ** 0.5
    upstream = cotangent.reshape(node_count, feat_width)
    weight_parts = [None] * layer_count
    bias_parts = [None] * layer_count
    for layer_no in reversed(range(layer_count)):
        layer_w = weights[layer_no]
        layer_b = biases[layer_no]
        (
            state_in,
            near_proj,
            far_table,
            pooled,
            message,
            node_pre,
            node_hidden,
            keep_msg,
            keep_node,
        ) = saved[layer_no]
        up_b = upstream.astype(jnp.bfloat16)
        grad_out_w = back_dot(node_hidden, up_b)
        d_pre = side_dot(up_b, layer_w[6]) * keep_node * silu_grad(node_pre)
        d_pre_b = d_pre.astype(jnp.bfloat16)
        grad_node_b = jnp.sum(d_pre, axis=0)
        grad_self_w = back_dot(state_in, d_pre_b)
        grad_msg_w = back_dot(message, d_pre_b)
        d_msg = (side_dot(d_pre_b, layer_w[3]) * keep_msg / slot_k).astype(jnp.bfloat16)
        grad_pool_w = back_dot(pooled, d_msg)
        d_pooled = side_dot(d_msg, layer_w[5]).astype(jnp.bfloat16)
        d_near, d_one, grad_mid_w, grad_mid_b, grad_edge_b = edge_backward(
            near_proj, far_table, row_index, valid_rows, layer_w[4], layer_b[1], d_pooled
        )
        far_buffer = (
            jnp.zeros(far_table.shape, jnp.float32)
            .at[row_index.reshape(-1)]
            .add(d_one.reshape(-1, feat_width))
        )
        d_far = fold_back(far_buffer.reshape(span_x + 2, span_y + 2, slots, feat_width)).reshape(
            node_count, feat_width
        )
        d_near_b = d_near.astype(jnp.bfloat16)
        d_far_b = d_far.astype(jnp.bfloat16)
        grad_near_w = back_dot(state_in, d_near_b)
        grad_far_w = back_dot(state_in, d_far_b)
        upstream = (
            upstream
            + side_dot(d_pre_b, layer_w[2])
            + side_dot(d_near_b, layer_w[0])
            + side_dot(d_far_b, layer_w[1])
        )
        local_w = jnp.stack(
            [grad_near_w, grad_far_w, grad_self_w, grad_msg_w, grad_mid_w, grad_pool_w, grad_out_w]
        )
        local_b = jnp.stack([grad_edge_b, grad_mid_b, grad_node_b])
        weight_parts[layer_no] = local_w
        bias_parts[layer_no] = local_b
    weight_total = jnp.stack(weight_parts)
    bias_total = jnp.stack(bias_parts)
    weight_total, bias_total = lax.psum((weight_total, bias_total), ("gx", "gy"))
    particle_grad = upstream.reshape(span_x, span_y, slots, feat_width)
    return (particle_grad, weight_total * norm_scale, bias_total * norm_scale)


def solution(mesh):
    in_specs = (
        P("gx", "gy", None, None),
        P("gx", "gy", None, None),
        P("gx", "gy", None, None),
        P(None, None, "gx", "gy", None, None),
        P(),
        P(),
        P("gx", "gy", None, None),
    )
    out_specs = (P("gx", "gy", None, None), P(), P())
    return jax.shard_map(shards, mesh=mesh, in_specs=in_specs, out_specs=out_specs, check_vma=False)
```

profile of v0, /device:TPU:1, one launch (start us, length us, event | category | flops | bytes accessed | tf_op | source)
XLA Modules:
  0.0 527.6 jit_solution(6338478000075864543)
XLA Ops:
  7.2 1.0 convolution_convert_fusion.3
  8.3 2.8 collective-permute-start
  11.7 1.0 fusion.85
  12.7 1.2 fusion.41
  14.0 0.8 slice_bitcast_fusion.6
  14.8 1.0 convolution_add_fusion.12
  15.8 1.0 fusion.137
  16.9 1.8 convert_multiply_fusion
  18.7 0.7 bitcast_convert_fusion
  19.5 1.1 collective-permute-start.2
  20.6 6.4 %collective-permute-start.3 = (bf16[6,1,16,128]{3,2,1,0:T(8,128)(2,1)S(1)}, bf16[6,1,16,128]{3,2,1,0:T(8,128)(2,1)S(1)}, u32[]{:S(2)}, u32[]{:S(2)}) collective-permute-start(bf16[6,1,16,128]{3,2,1,0:T(8,128)(2,1)S(1)} %get-tuple-element.140), channel_id=1, source_target_pairs={{1,0},{2,1},{3,2},{4,3},{5,4},{6,5},{7,6},{8,7},{9,8},{10,9},{11,1... | collective-permute-start | bytes 73736 | tf_op jit(solution)/shard_map/ppermute | solution.py:18
  27.1 1.0 collective-permute-done.2
  28.1 12.1 %gather_fusion = bf16[4096,128]{1,0:T(8,128)(2,1)S(1)} fusion(bf16[576,128]{1,0:T(8,128)(2,1)S(1)} %bitcast.346, s32[4096]{0:T(1024)S(1)} %fusion.125), kind=kCustom, calls=%fused_computation.clone | custom fusion | bytes 2113536 | tf_op jit(solution)/shard_map/jit(_take)/gather | solution.py:51
  40.3 1.1 multiply_convert_fusion.3
  41.3 2.0 multiply_convert_fusion.2
  43.9 0.8 fusion.43
  45.7 2.1 collective-permute-start.4
  47.8 1.9 collective-permute-start.5
  49.7 0.8 convolution_add_fusion.9
  51.1 6.3 %collective-permute-start.7 = (bf16[6,1,16,128]{3,2,1,0:T(8,128)(2,1)S(1)}, bf16[6,1,16,128]{3,2,1,0:T(8,128)(2,1)S(1)}, u32[]{:S(2)}, u32[]{:S(2)}) collective-permute-start(bf16[6,1,16,128]{3,2,1,0:T(8,128)(2,1)S(1)} %get-tuple-element.138), channel_id=1, source_target_pairs={{1,0},{2,1},{3,2},{4,3},{5,4},{6,5},{7,6},{8,7},{9,8},{10,9},{11,1... | collective-permute-start | bytes 73736 | tf_op jit(solution)/shard_map/ppermute | solution.py:18
  57.4 0.8 fusion.71
  58.4 12.1 %gather_fusion.1 = bf16[4096,128]{1,0:T(8,128)(2,1)S(1)} fusion(bf16[576,128]{1,0:T(8,128)(2,1)S(1)} %bitcast.345, s32[4096]{0:T(1024)S(1)} %fusion.125), kind=kCustom, calls=%fused_computation.1.clone | custom fusion | bytes 2113536 | tf_op jit(solution)/shard_map/jit(_take)/gather | solution.py:51
  70.5 3.1 select_convert_fusion.1
  73.7 1.0 multiply_convert_fusion.1
  76.2 0.8 fusion.44
  78.5 1.5 fusion.131
  80.0 2.5 fusion.128
  82.5 2.6 copy.65
  85.1 22.7 %scatter_custom_fusion = f32[576,128]{1,0:T(8,128)S(1)} fusion(s32[4096]{0:T(1024)S(1)} %bitcast.391, f32[4096,128]{1,0:T(8,128)} %bitcast.356, f32[]{:T(128)} %constant.266.clone.1), kind=kCustom, calls=%fused_computation.103 | custom fusion | flops 524288 | bytes 295424 | tf_op jit(solution)/shard_map/scatter-add | solution.py:214
  107.9 4.3 collective-permute-start.8
  112.2 1.2 convolution_add_fusion.7
  113.4 1.0 convolution_add_fusion.6
  114.5 1.0 collective-permute-done.9
  115.6 5.8 %collective-permute-start.10 = (bf16[4,16,128]{2,1,0:T(8,128)(2,1)S(1)}, bf16[4,16,128]{2,1,0:T(8,128)(2,1)S(1)}, u32[]{:S(2)}, u32[]{:S(2)}) collective-permute-start(bf16[4,16,128]{2,1,0:T(8,128)(2,1)S(1)} %get-tuple-element.136), channel_id=1, source_target_pairs={{1,0},{2,1},{3,2},{4,3},{5,4},{6,5},{7,6},{8,7},{9,8},{10,9},{11,1... | collective-permute-start | bytes 49160 | tf_op jit(solution)/shard_map/ppermute | solution.py:28
  121.4 0.9 fusion.23
  122.6 6.2 %collective-permute-done.11 = bf16[4,16,128]{2,1,0:T(8,128)(2,1)S(1)} collective-permute-done((bf16[4,16,128]{2,1,0:T(8,128)(2,1)S(1)}, bf16[4,16,128]{2,1,0:T(8,128)(2,1)S(1)}, u32[]{:S(2)}, u32[]{:S(2)}) %collective-permute-start.11) | collective-permute-done | bytes 16416 | tf_op jit(solution)/shard_map/ppermute | solution.py:28
  128.8 0.9 convolution_add_fusion.5
  129.8 1.5 fusion.135
  131.3 1.1 fusion.13
  132.3 1.6 convolution_add_fusion.4
  134.0 0.9 fusion.14
  134.9 1.5 fusion.129
  136.5 3.3 fusion.127
  139.7 2.6 copy.72
  142.3 22.7 %scatter_custom_fusion.1 = f32[576,128]{1,0:T(8,128)S(1)} fusion(s32[4096]{0:T(1024)S(1)} %bitcast.392, f32[4096,128]{1,0:T(8,128)} %bitcast.355, f32[]{:T(128)} %constant.266.clone.1), kind=kCustom, calls=%fused_computation.101 | custom fusion | flops 524288 | bytes 295424 | tf_op jit(solution)/shard_map/scatter-add | solution.py:214
  165.2 6.2 %collective-permute-start.12 = (bf16[6,16,128]{2,1,0:T(8,128)(2,1)S(1)}, bf16[6,16,128]{2,1,0:T(8,128)(2,1)}, u32[]{:S(2)}, u32[]{:S(2)}) collective-permute-start(bf16[6,16,128]{2,1,0:T(8,128)(2,1)S(1)} %bitcast.388), channel_id=1, source_target_pairs={{16,0},{32,16},{48,32},{64,48},{80,64},{96,80},{112,96},{128,112},... | collective-permute-start | bytes 73736 | tf_op jit(solution)/shard_map/ppermute | solution.py:28
  171.4 1.7 fusion.30
  173.1 1.7 fusion.22
  174.8 1.7 fusion.21
  176.4 1.7 fusion.20
  178.2 1.1 fusion.19
  179.3 0.9 fusion.18
  180.2 0.8 fusion.17
  181.1 74.8 %psum.15 = f32[2,3,128]{2,1,0:T(4,128)S(1)} all-reduce(f32[2,3,128]{2,1,0:T(4,128)S(1)} %pad_maximum_fusion.9), channel_id=1, replica_groups=mesh['gx'=16,'gy'=16] {'gx','gy'}, use_global_device_ids=true, to_apply=%region_11.13 | all-reduce | flops 768 | bytes 6144 | tf_op jit(solution)/shard_map/psum | solution.py:237
  255.9 0.7 bitcast_dynamic-update-slice_fusion
  256.6 0.7 fusion.51
  257.5 2.7 collective-permute-start.14
  261.0 6.0 %collective-permute-done.15 = bf16[4,16,128]{2,1,0:T(8,128)(2,1)S(1)} collective-permute-done((bf16[4,16,128]{2,1,0:T(8,128)(2,1)S(1)}, bf16[4,16,128]{2,1,0:T(8,128)(2,1)S(1)}, u32[]{:S(2)}, u32[]{:S(2)}) %collective-permute-start.15) | collective-permute-done | bytes 16416 | tf_op jit(solution)/shard_map/ppermute | solution.py:28
  268.7 1.0 pad_maximum_fusion
  269.8 0.9 convolution_add_fusion.3
  270.7 1.6 convolution_add_fusion.2
  272.3 246.0 %all-reduce.2.cloned.1.call-done = f32[2,7,128,128]{2,3,1,0:T(8,128)} async-done(((f32[2,7,128,128]{2,3,1,0:T(8,128)}), f32[2,7,128,128]{2,3,1,0:T(8,128)}) %all-reduce.2.cloned.1.call-update) | async-done | bytes 917520 | tf_op jit(solution)/shard_map/psum | solution.py:237
  518.3 1.2 broadcast_multiply_fusion
  519.6 1.2 copy.89
  (186 shorter events, 9.2 us)
Async XLA Ops:
  7.2 11.5 %copy-start.25 = (f32[4,4,16,128]{3,2,1,0:T(8,128)S(1)}, f32[4,4,16,128]{3,2,1,0:T(8,128)}, u32[]{:S(2)}) copy-start(f32[4,4,16,128]{3,2,1,0:T(8,128)} %param.31) | copy-start | bytes 393220
  7.2 511.1 %all-reduce.2.cloned.1.call-start = ((), (), s32[]{:S(2)}) async-start(), calls=%async_computation | async-start | bytes 1835008 | tf_op jit(solution)/shard_map/psum | solution.py:237
  8.3 11.2 %collective-permute-start = (bf16[1,4,16,128]{3,2,1,0:T(8,128)(2,1)S(1)}, bf16[1,4,16,128]{3,2,1,0:T(8,128)(2,1)S(1)}, u32[]{:S(2)}, u32[]{:S(2)}) collective-permute-start(bf16[1,4,16,128]{3,2,1,0:T(8,128)(2,1)S(1)} %bitcast.394), channel_id=1, source_target_pairs={{0,16},{16,32},{32,48},{48,64},{64,80},{80,96},{96,112},{112,128},... | collective-permute-start | bytes 49160 | tf_op jit(solution)/shard_map/ppermute | solution.py:16
  11.0 8.5 %collective-permute-start.1 = (bf16[1,4,16,128]{3,2,1,0:T(8,128)(2,1)S(1)}, bf16[1,4,16,128]{3,2,1,0:T(8,128)(2,1)S(1)}, u32[]{:S(2)}, u32[]{:S(2)}) collective-permute-start(bf16[1,4,16,128]{3,2,1,0:T(8,128)(2,1)S(1)} %bitcast.393), channel_id=1, source_target_pairs={{16,0},{32,16},{48,32},{64,48},{80,64},{96,80},{112,96},{128,112},... | collective-permute-start | bytes 49160 | tf_op jit(solution)/shard_map/ppermute | solution.py:18
  15.8 24.4 %copy-start.22 = (f32[256,128]{1,0:T(8,128)}, f32[256,128]{1,0:T(8,128)S(1)}, u32[]{:S(2)}) copy-start(f32[256,128]{1,0:T(8,128)S(1)} %convolution_add_fusion.12) | copy-start | bytes 393220
  16.9 26.5 %copy-start.44 = (bf16[4,4,16,16]{3,2,1,0:T(8,128)(2,1)}, bf16[4,4,16,16]{3,2,1,0:T(8,128)(2,1)S(1)}, u32[]{:S(2)}) copy-start(bf16[4,4,16,16]{3,2,1,0:T(8,128)(2,1)S(1)} %get-tuple-element.132) | copy-start | bytes 24580
  18.7 25.1 %copy-start.8 = (f32[1,1,4,4,16,128]{5,4,3,2,1,0:T(8,128)}, f32[1,1,4,4,16,128]{5,4,3,2,1,0:T(8,128)S(1)}, u32[]{:S(2)}) copy-start(f32[1,1,4,4,16,128]{5,4,3,2,1,0:T(8,128)S(1)} %get-tuple-element.118) | copy-start | bytes 393220
  18.7 25.2 %copy-start.40 = (f32[1,1,4,4,16,128]{5,4,3,2,1,0:T(8,128)}, f32[1,1,4,4,16,128]{5,4,3,2,1,0:T(8,128)S(1)}, u32[]{:S(2)}) copy-start(f32[1,1,4,4,16,128]{5,4,3,2,1,0:T(8,128)S(1)} %get-tuple-element.120) | copy-start | bytes 393220
  19.5 8.6 %collective-permute-start.2 = (bf16[6,1,16,128]{3,2,1,0:T(8,128)(2,1)S(1)}, bf16[6,1,16,128]{3,2,1,0:T(8,128)(2,1)S(1)}, u32[]{:S(2)}, u32[]{:S(2)}) collective-permute-start(bf16[6,1,16,128]{3,2,1,0:T(8,128)(2,1)S(1)} %get-tuple-element.139), channel_id=1, source_target_pairs={{0,1},{1,2},{2,3},{3,4},{4,5},{5,6},{6,7},{7,8},{8,9},{9,10},{10,1... | collective-permute-start | bytes 73736 | tf_op jit(solution)/shard_map/ppermute | solution.py:16
  20.6 7.5 %collective-permute-start.3 = (bf16[6,1,16,128]{3,2,1,0:T(8,128)(2,1)S(1)}, bf16[6,1,16,128]{3,2,1,0:T(8,128)(2,1)S(1)}, u32[]{:S(2)}, u32[]{:S(2)}) collective-permute-start(bf16[6,1,16,128]{3,2,1,0:T(8,128)(2,1)S(1)} %get-tuple-element.140), channel_id=1, source_target_pairs={{1,0},{2,1},{3,2},{4,3},{5,4},{6,5},{7,6},{8,7},{9,8},{10,9},{11,1... | collective-permute-start | bytes 73736 | tf_op jit(solution)/shard_map/ppermute | solution.py:18
  43.3 2.0 copy-start.2
  43.7 14.6 %copy-start.26 = (f32[256,1,128]{2,1,0:T(1,128)}, f32[256,1,128]{2,1,0:T(1,128)S(1)}, u32[]{:S(2)}) copy-start(f32[256,1,128]{2,1,0:T(1,128)S(1)} %fusion.49) | copy-start | bytes 393220
  43.9 14.4 %copy-start.33 = (bf16[256,128]{1,0:T(8,128)(2,1)}, bf16[256,128]{1,0:T(8,128)(2,1)S(1)}, u32[]{:S(2)}) copy-start(bf16[256,128]{1,0:T(8,128)(2,1)S(1)} %fusion.10) | copy-start | bytes 196612
  45.7 4.8 collective-permute-start.4
  47.8 3.2 collective-permute-start.5
  51.0 7.3 %collective-permute-start.6 = (bf16[6,1,16,128]{3,2,1,0:T(8,128)(2,1)S(1)}, bf16[6,1,16,128]{3,2,1,0:T(8,128)(2,1)S(1)}, u32[]{:S(2)}, u32[]{:S(2)}) collective-permute-start(bf16[6,1,16,128]{3,2,1,0:T(8,128)(2,1)S(1)} %get-tuple-element.137), channel_id=1, source_target_pairs={{0,1},{1,2},{2,3},{3,4},{4,5},{5,6},{6,7},{7,8},{8,9},{9,10},{10,1... | collective-permute-start | bytes 73736 | tf_op jit(solution)/shard_map/ppermute | solution.py:16
  51.1 7.2 %collective-permute-start.7 = (bf16[6,1,16,128]{3,2,1,0:T(8,128)(2,1)S(1)}, bf16[6,1,16,128]{3,2,1,0:T(8,128)(2,1)S(1)}, u32[]{:S(2)}, u32[]{:S(2)}) collective-permute-start(bf16[6,1,16,128]{3,2,1,0:T(8,128)(2,1)S(1)} %get-tuple-element.138), channel_id=1, source_target_pairs={{1,0},{2,1},{3,2},{4,3},{5,4},{6,5},{7,6},{8,7},{9,8},{10,9},{11,1... | collective-permute-start | bytes 73736 | tf_op jit(solution)/shard_map/ppermute | solution.py:18
  70.5 3.2 copy-start.24
  74.7 1.4 copy-start.39
  74.7 1.4 copy-start.42
  75.5 1.5 copy-start.46
  76.1 1.9 copy-start.36
  107.9 13.5 %copy-start.38 = (bf16[256,128]{1,0:T(8,128)(2,1)S(1)}, bf16[256,128]{1,0:T(8,128)(2,1)}, u32[]{:S(2)}) copy-start(bf16[256,128]{1,0:T(8,128)(2,1)} %get-tuple-element.112) | copy-start | bytes 196612
  107.9 21.9 %copy-start.41 = (f32[1,1,4,4,16,128]{5,4,3,2,1,0:T(8,128)S(1)}, f32[1,1,4,4,16,128]{5,4,3,2,1,0:T(8,128)}, u32[]{:S(2)}) copy-start(f32[1,1,4,4,16,128]{5,4,3,2,1,0:T(8,128)} %copy-done.40) | copy-start | bytes 393220
  107.9 21.9 %copy-start.53 = (f32[256,128]{1,0:T(8,128)S(1)}, f32[256,128]{1,0:T(8,128)}, u32[]{:S(2)}) copy-start(f32[256,128]{1,0:T(8,128)} %get-tuple-element.156) | copy-start | bytes 393220
  107.9 6.5 %collective-permute-start.8 = (bf16[6,16,128]{2,1,0:T(8,128)(2,1)S(1)}, bf16[6,16,128]{2,1,0:T(8,128)(2,1)S(1)}, u32[]{:S(2)}, u32[]{:S(2)}) collective-permute-start(bf16[6,16,128]{2,1,0:T(8,128)(2,1)S(1)} %bitcast.390), channel_id=1, source_target_pairs={{16,0},{32,16},{48,32},{64,48},{80,64},{96,80},{112,96},{128,112},... | collective-permute-start | bytes 73736 | tf_op jit(solution)/shard_map/ppermute | solution.py:28
  112.2 3.3 collective-permute-start.9
  112.2 19.0 %copy-start.9 = (f32[1,1,4,4,16,128]{5,4,3,2,1,0:T(8,128)S(1)}, f32[1,1,4,4,16,128]{5,4,3,2,1,0:T(8,128)}, u32[]{:S(2)}) copy-start(f32[1,1,4,4,16,128]{5,4,3,2,1,0:T(8,128)} %copy-done.8) | copy-start | bytes 393220
  114.4 20.5 %copy-start.4 = (f32[4096,128]{1,0:T(8,128)S(1)}, f32[4096,128]{1,0:T(8,128)}, u32[]{:S(2)}) copy-start(f32[4096,128]{1,0:T(8,128)} %get-tuple-element.154) | copy-start | bytes 6291460
  115.6 7.0 %collective-permute-start.10 = (bf16[4,16,128]{2,1,0:T(8,128)(2,1)S(1)}, bf16[4,16,128]{2,1,0:T(8,128)(2,1)S(1)}, u32[]{:S(2)}, u32[]{:S(2)}) collective-permute-start(bf16[4,16,128]{2,1,0:T(8,128)(2,1)S(1)} %get-tuple-element.136), channel_id=1, source_target_pairs={{1,0},{2,1},{3,2},{4,3},{5,4},{6,5},{7,6},{8,7},{9,8},{10,9},{11,1... | collective-permute-start | bytes 49160 | tf_op jit(solution)/shard_map/ppermute | solution.py:28
  122.2 6.5 %collective-permute-start.11 = (bf16[4,16,128]{2,1,0:T(8,128)(2,1)S(1)}, bf16[4,16,128]{2,1,0:T(8,128)(2,1)S(1)}, u32[]{:S(2)}, u32[]{:S(2)}) collective-permute-start(bf16[4,16,128]{2,1,0:T(8,128)(2,1)S(1)} %get-tuple-element.135), channel_id=1, source_target_pairs={{15,0},{0,1},{1,2},{2,3},{3,4},{4,5},{5,6},{6,7},{7,8},{8,9},{9,10... | collective-permute-start | bytes 49160 | tf_op jit(solution)/shard_map/ppermute | solution.py:28
  128.8 6.1 %copy-start.17 = (bf16[4,4,16,128]{3,2,1,0:T(8,128)(2,1)}, bf16[4,4,16,128]{3,2,1,0:T(8,128)(2,1)S(1)}, u32[]{:S(2)}) copy-start(bf16[4,4,16,128]{3,2,1,0:T(8,128)(2,1)S(1)} %copy.69) | copy-start | bytes 196612
  129.7 5.1 copy-start.6
  131.2 3.6 copy-start.11
  131.2 5.2 copy-start.5
  131.2 5.2 copy-start.23
  132.3 2.6 copy-start.20
  136.5 3.3 copy-start
  165.1 14.2 %copy-start.19 = (bf16[256,128]{1,0:T(8,128)(2,1)S(1)}, bf16[256,128]{1,0:T(8,128)(2,1)}, u32[]{:S(2)}) copy-start(bf16[256,128]{1,0:T(8,128)(2,1)} %copy-done.18) | copy-start | bytes 196612
  165.1 14.2 %copy-start.29 = (f32[256,1,128]{2,1,0:T(1,128)S(1)}, f32[256,1,128]{2,1,0:T(1,128)}, u32[]{:S(2)}) copy-start(f32[256,1,128]{2,1,0:T(1,128)} %copy-done.28) | copy-start | bytes 393220
  165.1 15.1 %copy-start.35 = (bf16[256,128]{1,0:T(8,128)(2,1)S(1)}, bf16[256,128]{1,0:T(8,128)(2,1)}, u32[]{:S(2)}) copy-start(bf16[256,128]{1,0:T(8,128)(2,1)} %get-tuple-element.129) | copy-start | bytes 196612
  165.1 15.1 %copy-start.43 = (bf16[256,128]{1,0:T(8,128)(2,1)S(1)}, bf16[256,128]{1,0:T(8,128)(2,1)}, u32[]{:S(2)}) copy-start(bf16[256,128]{1,0:T(8,128)(2,1)} %get-tuple-element.163) | copy-start | bytes 196612
  165.1 15.9 %copy-start.47 = (f32[128]{0:T(128)S(1)}, f32[128]{0:T(128)}, u32[]{:S(2)}) copy-start(f32[128]{0:T(128)} %get-tuple-element.115) | copy-start | bytes 1540
  165.1 15.9 %copy-start.48 = (f32[128]{0:T(128)S(1)}, f32[128]{0:T(128)}, u32[]{:S(2)}) copy-start(f32[128]{0:T(128)} %get-tuple-element.113) | copy-start | bytes 1540
  165.1 15.9 %copy-start.49 = (f32[128]{0:T(128)S(1)}, f32[128]{0:T(128)}, u32[]{:S(2)}) copy-start(f32[128]{0:T(128)} %get-tuple-element.127) | copy-start | bytes 1540
  165.1 15.9 %copy-start.50 = (f32[128]{0:T(128)S(1)}, f32[128]{0:T(128)}, u32[]{:S(2)}) copy-start(f32[128]{0:T(128)} %get-tuple-element.111) | copy-start | bytes 1540
  165.1 15.9 %copy-start.51 = (f32[128]{0:T(128)S(1)}, f32[128]{0:T(128)}, u32[]{:S(2)}) copy-start(f32[128]{0:T(128)} %get-tuple-element.125) | copy-start | bytes 1540
  165.1 15.9 %copy-start.52 = (f32[128]{0:T(128)S(1)}, f32[128]{0:T(128)}, u32[]{:S(2)}) copy-start(f32[128]{0:T(128)} %get-tuple-element.109) | copy-start | bytes 1540
  165.2 90.7 %collective-permute-start.12 = (bf16[6,16,128]{2,1,0:T(8,128)(2,1)S(1)}, bf16[6,16,128]{2,1,0:T(8,128)(2,1)}, u32[]{:S(2)}, u32[]{:S(2)}) collective-permute-start(bf16[6,16,128]{2,1,0:T(8,128)(2,1)S(1)} %bitcast.388), channel_id=1, source_target_pairs={{16,0},{32,16},{48,32},{64,48},{80,64},{96,80},{112,96},{128,112},... | collective-permute-start | bytes 73736 | tf_op jit(solution)/shard_map/ppermute | solution.py:28
  171.4 85.3 %collective-permute-start.13 = (bf16[6,16,128]{2,1,0:T(8,128)(2,1)S(1)}, bf16[6,16,128]{2,1,0:T(8,128)(2,1)}, u32[]{:S(2)}, u32[]{:S(2)}) collective-permute-start(bf16[6,16,128]{2,1,0:T(8,128)(2,1)S(1)} %bitcast.387), channel_id=1, source_target_pairs={{240,0},{0,16},{16,32},{32,48},{48,64},{64,80},{80,96},{96,112},{1... | collective-permute-start | bytes 73736 | tf_op jit(solution)/shard_map/ppermute | solution.py:28
  179.3 87.8 %copy-start.3 = (bf16[4,4,16,128]{3,2,1,0:T(8,128)(2,1)S(1)}, bf16[4,4,16,128]{3,2,1,0:T(8,128)(2,1)}, u32[]{:S(2)}) copy-start(bf16[4,4,16,128]{3,2,1,0:T(8,128)(2,1)} %param.25) | copy-start | bytes 196612
  179.3 87.8 %copy-start.15 = (f32[7,128,128]{1,2,0:T(8,128)S(1)}, f32[7,128,128]{1,2,0:T(8,128)}, u32[]{:S(2)}) copy-start(f32[7,128,128]{1,2,0:T(8,128)} %fusion.30) | copy-start | bytes 1376260
  179.3 88.0 %copy-start.12 = (bf16[256,128]{1,0:T(8,128)(2,1)S(1)}, bf16[256,128]{1,0:T(8,128)(2,1)}, u32[]{:S(2)}) copy-start(bf16[256,128]{1,0:T(8,128)(2,1)} %copy-done.11) | copy-start | bytes 196612
  179.3 88.2 %copy-start.34 = (bf16[256,128]{1,0:T(8,128)(2,1)S(1)}, bf16[256,128]{1,0:T(8,128)(2,1)}, u32[]{:S(2)}) copy-start(bf16[256,128]{1,0:T(8,128)(2,1)} %copy-done.33) | copy-start | bytes 196612
  179.3 88.4 %copy-start.1 = (bf16[4096,128]{1,0:T(8,128)(2,1)S(1)}, bf16[4096,128]{1,0:T(8,128)(2,1)}, u32[]{:S(2)}) copy-start(bf16[4096,128]{1,0:T(8,128)(2,1)} %copy-done) | copy-start | bytes 3145732
  257.4 10.8 %copy-start.21 = (bf16[256,128]{1,0:T(8,128)(2,1)S(1)}, bf16[256,128]{1,0:T(8,128)(2,1)}, u32[]{:S(2)}) copy-start(bf16[256,128]{1,0:T(8,128)(2,1)} %copy-done.20) | copy-start | bytes 196612
  257.4 10.8 %copy-start.27 = (f32[256,1,128]{2,1,0:T(1,128)S(1)}, f32[256,1,128]{2,1,0:T(1,128)}, u32[]{:S(2)}) copy-start(f32[256,1,128]{2,1,0:T(1,128)} %copy-done.26) | copy-start | bytes 393220
  257.4 11.0 %copy-start.7 = (f32[256,128]{1,0:T(8,128)S(1)}, f32[256,128]{1,0:T(8,128)}, u32[]{:S(2)}) copy-start(f32[256,128]{1,0:T(8,128)} %copy-done.6) | copy-start | bytes 393220
  257.4 11.0 %copy-start.32 = (bf16[256,128]{1,0:T(8,128)(2,1)S(1)}, bf16[256,128]{1,0:T(8,128)(2,1)}, u32[]{:S(2)}) copy-start(bf16[256,128]{1,0:T(8,128)(2,1)} %copy-done.31) | copy-start | bytes 196612
  257.5 3.5 collective-permute-start.14
  260.7 8.0 %copy-start.16 = (f32[7,128,128]{1,2,0:T(8,128)S(1)}, f32[7,128,128]{1,2,0:T(8,128)}, u32[]{:S(2)}) copy-start(f32[7,128,128]{1,2,0:T(8,128)} %fusion.17) | copy-start | bytes 1376260
  260.8 6.3 %collective-permute-start.15 = (bf16[4,16,128]{2,1,0:T(8,128)(2,1)S(1)}, bf16[4,16,128]{2,1,0:T(8,128)(2,1)S(1)}, u32[]{:S(2)}, u32[]{:S(2)}) collective-permute-start(bf16[4,16,128]{2,1,0:T(8,128)(2,1)S(1)} %get-tuple-element.133), channel_id=1, source_target_pairs={{15,0},{0,1},{1,2},{2,3},{3,4},{4,5},{5,6},{6,7},{7,8},{8,9},{9,10... | collective-permute-start | bytes 49160 | tf_op jit(solution)/shard_map/ppermute | solution.py:28
  268.2 1.5 copy-start.30
  268.2 1.5 copy-start.37
  (7 other events, 5.9 us)
Sparse Core Ops, SparseCore 0:
  269.9 248.4 all-reduce.1
where the time goes:
time: 529 us; the launch traced here: 528 us
  waiting for transfers between devices  261 us (49%)
  blocking collectives  74.8 us (14%)
  other arithmetic  62.5 us (12%)
  starting transfers between devices  40.6 us (8%)
  matrix products  39.8 us (8%)
  local copies, waits for them, and re-layouts  33.8 us (6%)
  between operations  15.1 us (3%)
    psum x1, waiting for transfers between devices, shards(): lax.psum((weight_total, bias_total), ('gx', 'gy'))  246 us
    psum x1, blocking collectives, shards(): lax.psum((weight_total, bias_total), ('gx', 'gy'))  74.8 us
    scatter-add x2, other arithmetic, shards(): far_buffer = jnp.zeros(far_table.shape, jnp.float32).at[row_index.reshape...  45.5 us
    gather x2, local copies, waits for them, and re-layouts, edge_forward(): jnp.take(far_table, row_index.reshape(-1), axis=0)  24.3 us
    ppermute x8, starting transfers between devices, shifted(): return lax.ppermute(block, axis, route)  19.4 us
    dot_general x14, matrix products, side_dot(): lax.dot_general(left_op, right_op, (((1,), (1,)), ((), ())), preferred_el...  17.5 us
    ppermute x4, starting transfers between devices, padded(): lax.ppermute(head, axis, [((i + 1) % count, i) for i in range(count)])  15.2 us
    ppermute x8, waiting for transfers between devices, shifted(): return lax.ppermute(block, axis, route)  13.4 us
  transfers between devices with their start and end apart: 17, of which 8 were waited for; matrix products, arithmetic and copies ran while one was open for 5% of the time, Pallas kernels for 0%

commit v1 on v0

v1 whole, which is shorter than its diff:
```python
import functools

import jax
import jax.experimental.pallas as pl
import jax.experimental.pallas.tpu as pltpu
import jax.numpy as jnp
from jax import lax
from jax.sharding import PartitionSpec as P

MESH = pl.DeviceIdType.MESH
BF16, F32 = jnp.bfloat16, jnp.float32
keep_scale = 10.0 / 9.0

Y_HI = 2
NEAR, FAR, SELF, MSG, MID, POOL, OUT = range(7)
EARLY = [(0, SELF), (0, MSG), (0, POOL), (0, OUT)] + [(1, m) for m in range(7)]
LATE = [(0, NEAR), (0, FAR), (0, MID)]
EARLY_TILES, LATE_TILES = 96, 32
BIAS_TILE = 24
ROUTES = [(1, 0), (-1, 0), (0, 1), (0, -1), (1, 1), (1, -1), (-1, 1), (-1, -1)]


def dot(a, b):
    return jnp.dot(a, b, preferred_element_type=F32)


def side_dot(a, b):
    return lax.dot_general(a, b, (((1,), (1,)), ((), ())), preferred_element_type=F32)


def back_dot(a, b):
    return lax.dot_general(a, b, (((0,), (0,)), ((), ())), preferred_element_type=F32)


def silu_parts(v):
    sig = 0.5 * jnp.tanh(0.5 * v) + 0.5
    value = v * sig
    return value, sig + value * (1.0 - sig)


def kernel(
    gx,
    gy,
    part_ref,
    code_ref,
    valid_ref,
    drop_ref,
    w_ref,
    b_ref,
    cot_ref,
    pgrad_ref,
    wgrad_ref,
    bgrad_ref,
    state_tab,
    far_tab,
    pick,
    place,
    group,
    valid_b,
    code_rows,
    near,
    g_one,
    g_two,
    first_t,
    pooled,
    message,
    hidden,
    g_node,
    d_pool,
    d_near,
    far_acc,
    far_send,
    far_recv,
    mid_acc,
    stage_e,
    rs_e,
    ar_e,
    ag_e,
    stage_l,
    rs_l,
    ar_l,
    ag_l,
    halo_send_sem,
    halo_recv_sem,
    back_send_sem,
    back_recv_sem,
    red_send_sem,
    red_recv_sem,
):
    me_x = lax.axis_index("gx")
    me_y = lax.axis_index("gy")
    depth = gy // Y_HI
    ring = gx * Y_HI
    me_z = lax.rem(me_y, depth)
    me_r = me_x * Y_HI + me_y // depth
    nodes = 256
    cells = 16

    barrier = pltpu.get_barrier_semaphore()

    def greet_ring(d, _):
        t = lax.rem(me_r + d, ring)
        pl.semaphore_signal(
            barrier,
            inc=1,
            device_id=(t // Y_HI, lax.rem(t, Y_HI) * depth + me_z),
            device_id_type=MESH,
        )
        return 0

    def greet_z(d, _):
        t = lax.rem(me_z + d, depth)
        pl.semaphore_signal(
            barrier, inc=1, device_id=(me_x, me_y - me_z + t), device_id_type=MESH
        )
        return 0

    def neighbour(dx, dy):
        return (lax.rem(me_x + dx + gx, gx), lax.rem(me_y + dy + gy, gy))

    for dx, dy in ROUTES:
        pl.semaphore_signal(barrier, inc=1, device_id=neighbour(dx, dy), device_id_type=MESH)
    lax.fori_loop(1, ring, greet_ring, 0)
    lax.fori_loop(1, depth, greet_z, 0)

    state_tab[0, 1:5, 1:5] = part_ref[...]

    spread = jnp.where(
        lax.broadcasted_iota(jnp.int32, (16, 256), 1) // 16
        == lax.broadcasted_iota(jnp.int32, (16, 256), 0),
        1.0,
        0.0,
    ).astype(BF16)
    own = jnp.where(
        lax.rem(lax.broadcasted_iota(jnp.int32, (nodes, 256), 0), 16)
        == lax.rem(lax.broadcasted_iota(jnp.int32, (nodes, 256), 1), 16),
        1.0,
        0.0,
    )
    gather_cell = jnp.where(
        lax.broadcasted_iota(jnp.int32, (cells, nodes), 1) // 16
        == lax.broadcasted_iota(jnp.int32, (cells, nodes), 0),
        1.0,
        0.0,
    ).astype(BF16)
    codes = code_ref[...].reshape(nodes, 16).astype(F32).astype(BF16)
    valid = valid_ref[...].reshape(nodes, 16).astype(F32).astype(BF16)
    code_rows[...] = dot(gather_cell, (dot(codes, spread) * own).astype(BF16))
    group[...] = (dot(valid, spread) * own).astype(BF16).reshape(cells, 16, 256)

    pl.semaphore_wait(barrier, ring - 1 + depth - 1 + len(ROUTES))

    def part(step, edge, width):
        return pl.ds(1, 4) if step == 0 else pl.ds(edge[0] if step > 0 else edge[1], width)

    def halo_copies(layer):
        copies = []
        for n, (dx, dy) in enumerate(ROUTES):
            tab = state_tab.at[layer]
            copies.append(
                pltpu.make_async_remote_copy(
                    src_ref=tab.at[part(dx, (4, 1), 1), part(dy, (4, 1), 1)],
                    dst_ref=tab.at[part(dx, (0, 5), 1), part(dy, (0, 5), 1)],
                    send_sem=halo_send_sem.at[layer, n],
                    recv_sem=halo_recv_sem.at[layer, n],
                    device_id=neighbour(dx, dy),
                    device_id_type=MESH,
                )
            )
        return copies

    def back_copies(layer):
        copies = []
        for n, (dx, dy) in enumerate(ROUTES):
            x = pl.ds(1, 4) if dx == 0 else (5 if dx > 0 else 0)
            y = pl.ds(1, 4) if dy == 0 else (5 if dy > 0 else 0)
            target = far_recv.at[layer, n]
            copies.append(
                pltpu.make_async_remote_copy(
                    src_ref=far_send.at[layer, x, y],
                    dst_ref=target.at[0] if dx and dy else target,
                    send_sem=back_send_sem.at[layer, n],
                    recv_sem=back_recv_sem.at[layer, n],
                    device_id=neighbour(dx, dy),
                    device_id_type=MESH,
                )
            )
        return copies

    halos = [halo_copies(layer) for layer in range(2)]
    backs = [back_copies(layer) for layer in range(2)]
    for copy in halos[0]:
        copy.start()

    slot_rows = lax.broadcasted_iota(jnp.int32, (144, 256), 0).astype(F32)
    slot_lanes = lax.broadcasted_iota(jnp.int32, (16, 256), 1).astype(F32)

    def prepare(c, _):
        row = code_rows[pl.ds(c, 1), :]
        place[c] = jnp.where(slot_rows == row, 1.0, 0.0).astype(BF16)
        code = code_ref[c].astype(F32)
        flag = valid_ref[c].astype(F32)
        for k in range(16):
            column = jnp.broadcast_to(code[:, k : k + 1], (16, 256))
            pick[c, k * 16 : (k + 1) * 16, :] = jnp.where(column == slot_lanes, 1.0, 0.0).astype(
                BF16
            )
            valid_b[c, k * 16 : (k + 1) * 16, :] = jnp.broadcast_to(
                flag[:, k : k + 1], (16, 128)
            ).astype(BF16)
        return 0

    lax.fori_loop(0, cells, prepare, 0)

    def matrix(layer, m):
        return w_ref[layer, m]

    def inner_state(layer):
        return state_tab[layer, 1:5, 1:5].reshape(nodes, 128)

    def forward(layer):
        state = inner_state(layer)
        near[...] = dot(state, matrix(layer, NEAR)) + b_ref[layer, 0:1, :]
        for copy in halos[layer]:
            copy.wait_recv()
        far = dot(state_tab[layer].reshape(576, 128), matrix(layer, FAR)).astype(BF16)
        far_tab[...] = far.reshape(6, 6, 16, 128)
        mid_w = matrix(layer, MID)
        mid_b = b_ref[layer, 1:2, :]

        def row(x, _):
            for y in range(4):
                c = x * 4 + y
                block = far_tab[pl.ds(x, 3), y : y + 3].reshape(144, 128)
                block = jnp.concatenate([block, jnp.zeros((112, 128), BF16)], axis=0)
                fetched = dot(pick[c], block)
                base = near[pl.ds(pl.multiple_of(c * 16, 16), 16), :]
                pre_one = (fetched.reshape(16, 16, 128) + base[None]).reshape(256, 128)
                value, slope = silu_parts(pre_one)
                first = value.astype(BF16)
                g_one[layer, c] = slope.astype(BF16)
                first_t[layer, c] = first.T
                pre_two = dot(first, mid_w) + mid_b
                value, slope = silu_parts(pre_two)
                g_two[layer, c] = (slope * valid_b[c].astype(F32)).astype(BF16)
                total = dot(group[c], value.astype(BF16))
                pooled[layer, pl.ds(pl.multiple_of(c * 16, 16), 16), :] = total.astype(BF16)
            return 0

        lax.fori_loop(0, 4, row, 0)
        keep_msg = drop_ref[2 * layer].astype(F32) * (keep_scale / 16)
        keep_node = drop_ref[2 * layer + 1].astype(F32) * keep_scale
        msg = (dot(pooled[layer], matrix(layer, POOL)) * keep_msg).astype(BF16)
        message[layer] = msg
        node_pre = (
            dot(state, matrix(layer, SELF)) + dot(msg, matrix(layer, MSG)) + b_ref[layer, 2:3, :]
        )
        value, slope = silu_parts(node_pre)
        node_hidden = (value * keep_node).astype(BF16)
        hidden[layer] = node_hidden
        g_node[layer] = slope * keep_node
        return state, node_hidden

    state, node_hidden = forward(0)
    after = (state.astype(F32) + dot(node_hidden, matrix(0, OUT))).astype(BF16)
    state_tab[1, 1:5, 1:5] = after.reshape(4, 4, 16, 128)
    for copy in halos[1]:
        copy.start()
    forward(1)

    def node_back(layer, up_b):
        d_pre = side_dot(up_b, matrix(layer, OUT)) * g_node[layer]
        d_pre_b = d_pre.astype(BF16)
        keep_msg = drop_ref[2 * layer].astype(F32) * (keep_scale / 16)
        d_msg = (side_dot(d_pre_b, matrix(layer, MSG)) * keep_msg).astype(BF16)
        d_pool[...] = side_dot(d_msg, matrix(layer, POOL)).astype(BF16)
        return d_pre_b, d_msg, jnp.sum(d_pre, axis=0, keepdims=True)

    def edges_back(layer):
        mid_w = matrix(layer, MID)
        far_acc[...] = jnp.zeros((6, 6, 16, 128), F32)
        mid_acc[...] = jnp.zeros((128, 128), F32)

        def row(x, mid_b_sum):
            for y in range(4):
                c = x * 4 + y
                rows = pl.ds(pl.multiple_of(c * 16, 16), 16)
                upper = d_pool[rows, :].astype(F32)
                d_two = g_two[layer, c].astype(F32).reshape(16, 16, 128) * upper[None]
                mid_b_sum = mid_b_sum + jnp.sum(d_two, axis=0)
                d_two_b = d_two.reshape(256, 128).astype(BF16)
                mid_acc[...] += dot(first_t[layer, c], d_two_b)
                d_one = side_dot(d_two_b, mid_w) * g_one[layer, c].astype(F32)
                d_near[rows, :] = jnp.sum(d_one.reshape(16, 16, 128), axis=0)
                spill = dot(place[c], d_one.astype(BF16))
                far_acc[pl.ds(x, 3), y : y + 3] += spill.reshape(3, 3, 16, 128)
            return mid_b_sum

        mid_b_sum = lax.fori_loop(0, 4, row, jnp.zeros((16, 128), F32))
        far_send[layer] = far_acc[...].astype(BF16)
        for copy in backs[layer]:
            copy.start()
        return jnp.sum(mid_b_sum, axis=0, keepdims=True)

    def finish_far(layer):
        for n, (dx, dy) in enumerate(ROUTES):
            backs[layer][n].wait_recv()
            x = pl.ds(1, 4) if dx == 0 else pl.ds(1 if dx > 0 else 4, 1)
            y = pl.ds(1, 4) if dy == 0 else pl.ds(1 if dy > 0 else 4, 1)
            block = far_recv[layer, n].astype(F32)
            if dx and dy:
                far_acc[x, y] += block[0:1][None]
            elif dx:
                far_acc[x, y] += block[None]
            else:
                far_acc[x, y] += block[:, None]
        return far_acc[1:5, 1:5].reshape(nodes, 128).astype(BF16)

    def put(stage, index, value):
        rows = stage.shape[1]
        flat = index * 128
        value = value.astype(BF16)
        done = 0
        while done < 128:
            p, offset = divmod(flat + done, rows)
            count = min(rows - offset, 128 - done)
            stage[p, offset : offset + count, :] = value[done : done + count]
            done += count

    def put_weight(layer, m, value):
        if (layer, m) in EARLY:
            put(stage_e, EARLY.index((layer, m)), value)
        else:
            put(stage_l, LATE.index((layer, m)), value)

    def edge_grads(layer):
        put_weight(layer, MID, mid_acc[...])
        near_b = d_near[...].astype(BF16)
        put_weight(layer, NEAR, back_dot(inner_state(layer), near_b))
        put_weight(
            layer,
            FAR,
            back_dot(state_tab[layer].reshape(576, 128), far_send[layer].reshape(576, 128)),
        )
        return near_b, jnp.sum(d_near[...], axis=0, keepdims=True)

    def node_grads(layer, up_b, d_pre_b, d_msg):
        put_weight(layer, OUT, back_dot(hidden[layer], up_b))
        put_weight(layer, SELF, back_dot(inner_state(layer), d_pre_b))
        put_weight(layer, MSG, back_dot(message[layer], d_pre_b))
        put_weight(layer, POOL, back_dot(pooled[layer], d_msg))

    def ring_device(t):
        return (t // Y_HI, lax.rem(t, Y_HI) * depth + me_z)

    def ring_send(source, target, n, fixed):
        def body(d, _):
            t = lax.rem(me_r + d, ring)
            pltpu.make_async_remote_copy(
                src_ref=source.at[me_r if fixed else t],
                dst_ref=target.at[me_r],
                send_sem=red_send_sem.at[n],
                recv_sem=red_recv_sem.at[n],
                device_id=ring_device(t),
                device_id_type=MESH,
            ).start()
            return 0

        lax.fori_loop(1, ring, body, 0)

    def z_send(buffer, n):
        def body(d, _):
            t = lax.rem(me_z + d, depth)
            pltpu.make_async_remote_copy(
                src_ref=buffer.at[me_z],
                dst_ref=buffer.at[me_z],
                send_sem=red_send_sem.at[n],
                recv_sem=red_recv_sem.at[n],
                device_id=(me_x, me_y - me_z + t),
                device_id_type=MESH,
            ).start()
            return 0

        lax.fori_loop(1, depth, body, 0)

    def wait_all(sem, buffer, count):
        view = buffer.at[pl.ds(0, count)]
        pltpu.make_async_copy(view, view, sem).wait()

    def fold(buffer, count):
        total = buffer[0].astype(F32)
        for n in range(1, count):
            total = total + buffer[n].astype(F32)
        return total

    late_per = LATE_TILES // ring

    def split_again(total, late):
        plain = total.astype(BF16)
        if not late:
            return plain
        tile = BIAS_TILE % late_per * 16
        both = total[tile : tile + 8] + total[tile + 8 : tile + 16]
        high = both.astype(BF16).astype(F32)
        pieces = [total[:tile], high, both - high, total[tile + 16 :]]
        fixed = jnp.concatenate([p for p in pieces if p.shape[0]], axis=0).astype(BF16)
        return jnp.where(me_r == BIAS_TILE // late_per, fixed, plain)

    def reduce_start(stage, rs, n):
        rs[me_r] = stage[me_r]
        ring_send(stage, rs, n, False)

    def reduce_across(rs, ar, n, late):
        wait_all(red_recv_sem.at[n], rs, ring - 1)
        ar[me_z] = split_again(fold(rs, ring), late)
        z_send(ar, n + 1)

    def reduce_share(ar, ag, n, late):
        wait_all(red_recv_sem.at[n + 1], ar, depth - 1)
        ag[me_r] = split_again(fold(ar, depth), late)
        ring_send(ag, ag, n + 2, True)

    upstream = cot_ref[...]
    up_b = upstream.astype(BF16)
    d_pre_b, d_msg, node_b1 = node_back(1, up_b)
    mid_b1 = edges_back(1)
    near_b, edge_b1 = edge_grads(1)
    node_grads(1, up_b, d_pre_b, d_msg)
    upstream = (
        upstream + side_dot(d_pre_b, matrix(1, SELF)) + side_dot(near_b, matrix(1, NEAR))
    )
    upstream = upstream + side_dot(finish_far(1), matrix(1, FAR))

    up_b = upstream.astype(BF16)
    d_pre_b, d_msg, node_b0 = node_back(0, up_b)
    node_grads(0, up_b, d_pre_b, d_msg)
    used = len(EARLY) * 128
    rows = stage_e.shape[1]
    while used < EARLY_TILES * 16:
        p, offset = divmod(used, rows)
        stage_e[p, offset:rows, :] = jnp.zeros((rows - offset, 128), BF16)
        used += rows - offset
    reduce_start(stage_e, rs_e, 0)
    mid_b0 = edges_back(0)
    near_b, edge_b0 = edge_grads(0)
    sums = jnp.concatenate(
        [edge_b0, mid_b0, node_b0, edge_b1, mid_b1, node_b1, jnp.zeros((2, 128), F32)], axis=0
    )
    high = sums.astype(BF16).astype(F32)
    rows = stage_l.shape[1]
    p, offset = divmod(BIAS_TILE * 16, rows)
    stage_l[p, offset : offset + 16, :] = jnp.concatenate([high, sums - high], axis=0).astype(BF16)
    used = (BIAS_TILE + 1) * 16
    while used < LATE_TILES * 16:
        p, offset = divmod(used, rows)
        stage_l[p, offset:rows, :] = jnp.zeros((rows - offset, 128), BF16)
        used += rows - offset
    reduce_start(stage_l, rs_l, 3)
    reduce_across(rs_e, ar_e, 0, False)
    upstream = (
        upstream + side_dot(d_pre_b, matrix(0, SELF)) + side_dot(near_b, matrix(0, NEAR))
    )
    pgrad_ref[...] = upstream + side_dot(finish_far(0), matrix(0, FAR))
    reduce_across(rs_l, ar_l, 3, True)
    reduce_share(ar_e, ag_e, 0, False)
    reduce_share(ar_l, ag_l, 3, True)

    def take(gathered, index):
        rows = gathered.shape[1]
        pieces = []
        done = 0
        while done < 128:
            p, offset = divmod(index * 128 + done, rows)
            count = min(rows - offset, 128 - done)
            pieces.append(gathered[p, offset : offset + count, :])
            done += count
        return jnp.concatenate(pieces, axis=0)

    wait_all(red_recv_sem.at[2], ag_e, ring - 1)
    for n, (layer, m) in enumerate(EARLY):
        wgrad_ref[layer, m] = take(ag_e, n)
    wait_all(red_recv_sem.at[5], ag_l, ring - 1)
    for n, (layer, m) in enumerate(LATE):
        wgrad_ref[layer, m] = take(ag_l, n)
    p, offset = divmod(BIAS_TILE * 16, ag_l.shape[1])
    pair = ag_l[p, offset : offset + 16, :].astype(F32)
    bgrad_ref[...] = pair[0:8] + pair[8:16]

    for layer in range(2):
        for copy in halos[layer] + backs[layer]:
            copy.wait_send()
    for n, buffer, count in (
        (0, rs_e, ring - 1),
        (1, ar_e, depth - 1),
        (2, ag_e, ring - 1),
        (3, rs_l, ring - 1),
        (4, ar_l, depth - 1),
        (5, ag_l, ring - 1),
    ):
        wait_all(red_send_sem.at[n], buffer, count)


def solution(mesh):
    gx, gy = mesh.shape["gx"], mesh.shape["gy"]
    ring, depth = gx * Y_HI, gy // Y_HI
    early, late = EARLY_TILES // ring * 16, LATE_TILES // ring * 16
    total_nodes = gx * gy * 256
    norm_scale = 1.0 / total_nodes**0.5

    def shards(particles, neighbours, edge_valid, dropout_keep, weights, biases, cotangent):
        vmem = pltpu.VMEM
        scratch = [
            vmem((2, 6, 6, 16, 128), BF16),
            vmem((6, 6, 16, 128), BF16),
            vmem((16, 256, 256), BF16),
            vmem((16, 144, 256), BF16),
            vmem((16, 16, 256), BF16),
            vmem((16, 256, 128), BF16),
            vmem((16, 256), F32),
            vmem((256, 128), F32),
            vmem((2, 16, 256, 128), BF16),
            vmem((2, 16, 256, 128), BF16),
            vmem((2, 16, 128, 256), BF16),
            vmem((2, 256, 128), BF16),
            vmem((2, 256, 128), BF16),
            vmem((2, 256, 128), BF16),
            vmem((2, 256, 128), F32),
            vmem((256, 128), BF16),
            vmem((256, 128), F32),
            vmem((6, 6, 16, 128), F32),
            vmem((2, 6, 6, 16, 128), BF16),
            vmem((2, 8, 4, 16, 128), BF16),
            vmem((128, 128), F32),
            vmem((ring, early, 128), BF16),
            vmem((ring, early, 128), BF16),
            vmem((depth, early, 128), BF16),
            vmem((ring, early, 128), BF16),
            vmem((ring, late, 128), BF16),
            vmem((ring, late, 128), BF16),
            vmem((depth, late, 128), BF16),
            vmem((ring, late, 128), BF16),
            pltpu.SemaphoreType.DMA((2, 8)),
            pltpu.SemaphoreType.DMA((2, 8)),
            pltpu.SemaphoreType.DMA((2, 8)),
            pltpu.SemaphoreType.DMA((2, 8)),
            pltpu.SemaphoreType.DMA((6,)),
            pltpu.SemaphoreType.DMA((6,)),
        ]
        whole = pl.BlockSpec(memory_space=pltpu.VMEM)
        pgrad, wgrad, bgrad = pl.pallas_call(
            functools.partial(kernel, gx, gy),
            out_shape=(
                jax.ShapeDtypeStruct((256, 128), F32),
                jax.ShapeDtypeStruct((2, 7, 128, 128), BF16),
                jax.ShapeDtypeStruct((8, 128), F32),
            ),
            in_specs=[whole] * 7,
            out_specs=(whole, whole, whole),
            scratch_shapes=scratch,
            compiler_params=pltpu.CompilerParams(
                collective_id=0, has_side_effects=True, vmem_limit_bytes=40 * 2**20
            ),
            name="evolver",
        )(
            particles,
            neighbours.reshape(16, 16, 16),
            edge_valid.reshape(16, 16, 16),
            dropout_keep.reshape(4, 256, 128),
            weights,
            biases,
            cotangent.reshape(256, 128),
        )
        return (
            pgrad.reshape(particles.shape),
            wgrad.astype(F32) * norm_scale,
            bgrad[:6].reshape(biases.shape) * norm_scale,
        )

    cells = P("gx", "gy", None, None)
    return jax.shard_map(
        shards,
        mesh=mesh,
        in_specs=(cells, cells, cells, P(None, None, "gx", "gy", None, None), P(), P(), cells),
        out_specs=(cells, P(), P()),
        check_vma=False,
    )
```

time: 529 us -> 72.9 us (0.14)
  waiting for transfers between devices: 261 us -> 0 us
  blocking collectives: 74.8 us -> 0 us
  Pallas kernels: 0 us -> 63.4 us
  other arithmetic: 62.5 us -> 1.02 us
  starting transfers between devices: 40.6 us -> 0 us
  matrix products: 39.8 us -> 0 us
  local copies, waits for them, and re-layouts: 33.8 us -> 7.53 us
  between operations: 15.1 us -> 0.66 us
    psum x1 -> x0, waiting for transfers between devices: 246 us -> none  [shards(): lax.psum((weight_total, bias_total), ('gx', 'gy'))]
    psum x1 -> x0, blocking collectives: 74.8 us -> none  [shards(): lax.psum((weight_total, bias_total), ('gx', 'gy'))]
    pallas_call x0 -> x1, Pallas kernels: none -> 63.4 us  [shards(): pl.pallas_call(functools.partial(kernel, gx, gy), out_shape=(jax.ShapeDty...]
    scatter-add x10 -> x0, other arithmetic: 47 us -> none  [the longest x2 45.5 us: shards(): far_buffer = jnp.zeros(far_table.shape, jnp.float32).at[row_index.reshape...]
    ppermute x16 -> x0, starting transfers between devices: 40.6 us -> none  [the longest x8 19.4 us: shifted(): return lax.ppermute(block, axis, route)]
    dot_general x43 -> x0, matrix products: 39.8 us -> none  [the longest x14 17.5 us: side_dot(): lax.dot_general(left_op, right_op, (((1,), (1,)), ((), ())), preferred_el...]
    gather x2 -> x0, local copies, waits for them, and re-layouts: 24.3 us -> none  [edge_forward(): jnp.take(far_table, row_index.reshape(-1), axis=0)]
    ppermute x16 -> x0, waiting for transfers between devices: 15 us -> none  [the longest x8 13.4 us: shifted(): return lax.ppermute(block, axis, route)]
  transfers between devices with their start and end apart: 17 -> 0, of which waited for: 8 -> 0; matrix products, arithmetic and copies ran while one was open for 5% -> 0% of each run, Pallas kernels for 0% -> 0%
where the time goes in v1:
time: 72.9 us; the launch traced here: 72.6 us
  Pallas kernels  63.4 us (87%)
  local copies, waits for them, and re-layouts  7.53 us (10%)
  other arithmetic  1.02 us (1%)
    pallas_call x1, Pallas kernels, shards(): pl.pallas_call(functools.partial(kernel, gx, gy), out_shape=(jax.ShapeDty...  63.4 us
    unnamed x17, local copies, waits for them, and re-layouts  7.52 us

profile of v1, /device:TPU:1, one launch (start us, length us, event | category | flops | bytes accessed | tf_op | source)
XLA Modules:
  0.0 72.6 jit_solution(5412670676533025233)
XLA Ops:
  0.6 0.0 copy-start.6
  0.6 0.7 copy-done.6
  1.3 0.0 copy-start
  1.3 1.0 %copy-done = s32[2,2,4,4,16,128]{5,4,3,2,1,0:T(8,128)S(1)} copy-done((s32[2,2,4,4,16,128]{5,4,3,2,1,0:T(8,128)S(1)}, s32[2,2,4,4,16,128]{5,4,3,2,1,0:T(8,128)}, u32[]{:S(2)}) %copy-start) | copy-done | bytes 524312
  2.4 0.0 copy-start.1
  2.4 1.0 %copy-done.1 = bf16[2,7,128,128]{3,2,1,0:T(8,128)(2,1)S(1)} copy-done((bf16[2,7,128,128]{3,2,1,0:T(8,128)(2,1)S(1)}, bf16[2,7,128,128]{3,2,1,0:T(8,128)(2,1)}, u32[]{:S(2)}) %copy-start.1) | copy-done | bytes 458776
  3.4 0.0 copy-start.2
  3.4 0.9 %copy-done.2 = s32[4,4,16,16]{3,2,1,0:T(8,128)S(1)} copy-done((s32[4,4,16,16]{3,2,1,0:T(8,128)S(1)}, s32[4,4,16,16]{3,2,1,0:T(8,128)}, u32[]{:S(2)}) %copy-start.2) | copy-done | bytes 16408
  4.3 0.0 copy-start.3
  4.3 0.9 %copy-done.3 = s32[4,4,16,16]{3,2,1,0:T(8,128)S(1)} copy-done((s32[4,4,16,16]{3,2,1,0:T(8,128)S(1)}, s32[4,4,16,16]{3,2,1,0:T(8,128)}, u32[]{:S(2)}) %copy-start.3) | copy-done | bytes 16408
  5.2 0.0 copy-start.4
  5.2 0.9 %copy-done.4 = f32[4,4,16,128]{3,2,1,0:T(8,128)S(1)} copy-done((f32[4,4,16,128]{3,2,1,0:T(8,128)S(1)}, f32[4,4,16,128]{3,2,1,0:T(8,128)}, u32[]{:S(2)}) %copy-start.4) | copy-done | bytes 131096
  6.1 0.0 copy-start.5
  6.1 0.8 %copy-done.5 = bf16[4,4,16,128]{3,2,1,0:T(8,128)(2,1)S(1)} copy-done((bf16[4,4,16,128]{3,2,1,0:T(8,128)(2,1)S(1)}, bf16[4,4,16,128]{3,2,1,0:T(8,128)(2,1)}, u32[]{:S(2)}) %copy-start.5) | copy-done | bytes 65560
  6.9 63.4 %evolver.1 = (f32[256,128]{1,0:T(8,128)S(1)}, bf16[2,7,128,128]{3,2,1,0:T(8,128)(2,1)S(1)}, f32[8,128]{1,0:T(8,128)S(1)}) custom-call(bf16[4,4,16,128]{3,2,1,0:T(8,128)(2,1)S(1)} %copy-done.5, s32[16,16,16]{2,1,0:T(8,128)S(1)} %bitcast.7, s32[16,16,16]{2,1,0:T(8,128)S(1)} %bitcast.8, s32[4,256,128]{2,1,0:T(8,128)S(1)} %bitcast.5, ...), custom_call_target="tpu_custom_call" | custom-call | tf_op jit(solution)/shard_map/evolver/pallas_call | solution.py:550
  70.3 0.6 copy.13
  70.9 1.0 %convert_multiply_fusion = f32[2,7,128,128]{3,2,1,0:T(8,128)} fusion(bf16[2,7,128,128]{3,2,1,0:T(8,128)(2,1)S(1)} %get-tuple-element.7), kind=kLoop, calls=%fused_computation | loop fusion | flops 458752 | bytes 1376256 | tf_op jit(solution)/shard_map/mul | solution.py:575
  71.9 0.7 copy.15
  (3 shorter events, 0.0 us)
Async XLA Ops:
  0.6 0.7 copy-start.6
  1.3 1.0 %copy-start = (s32[2,2,4,4,16,128]{5,4,3,2,1,0:T(8,128)S(1)}, s32[2,2,4,4,16,128]{5,4,3,2,1,0:T(8,128)}, u32[]{:S(2)}) copy-start(s32[2,2,4,4,16,128]{5,4,3,2,1,0:T(8,128)} %param.10) | copy-start | bytes 1572868
  2.4 1.0 %copy-start.1 = (bf16[2,7,128,128]{3,2,1,0:T(8,128)(2,1)S(1)}, bf16[2,7,128,128]{3,2,1,0:T(8,128)(2,1)}, u32[]{:S(2)}) copy-start(bf16[2,7,128,128]{3,2,1,0:T(8,128)(2,1)} %w_ref.1) | copy-start | bytes 1376260
  3.4 0.9 %copy-start.2 = (s32[4,4,16,16]{3,2,1,0:T(8,128)S(1)}, s32[4,4,16,16]{3,2,1,0:T(8,128)}, u32[]{:S(2)}) copy-start(s32[4,4,16,16]{3,2,1,0:T(8,128)} %param.8) | copy-start | bytes 49156
  4.3 0.9 %copy-start.3 = (s32[4,4,16,16]{3,2,1,0:T(8,128)S(1)}, s32[4,4,16,16]{3,2,1,0:T(8,128)}, u32[]{:S(2)}) copy-start(s32[4,4,16,16]{3,2,1,0:T(8,128)} %param.9) | copy-start | bytes 49156
  5.2 0.9 %copy-start.4 = (f32[4,4,16,128]{3,2,1,0:T(8,128)S(1)}, f32[4,4,16,128]{3,2,1,0:T(8,128)}, u32[]{:S(2)}) copy-start(f32[4,4,16,128]{3,2,1,0:T(8,128)} %param.13) | copy-start | bytes 393220
  6.1 0.8 %copy-start.5 = (bf16[4,4,16,128]{3,2,1,0:T(8,128)(2,1)S(1)}, bf16[4,4,16,128]{3,2,1,0:T(8,128)(2,1)}, u32[]{:S(2)}) copy-start(bf16[4,4,16,128]{3,2,1,0:T(8,128)(2,1)} %part_ref.1) | copy-start | bytes 196612

commit v2 on v1

--- a/solution.py
+++ b/solution.py
@@ -72,6 +72,7 @@
     far_send,
     far_recv,
     mid_acc,
+    mid_pair,
     stage_e,
     rs_e,
     ar_e,
@@ -212,6 +213,17 @@
 
     lax.fori_loop(0, cells, prepare, 0)
 
+    empty = jnp.zeros((128, 128), BF16)
+    for layer in range(2):
+        mid_w = w_ref[layer, MID]
+        mid_pair[layer] = jnp.concatenate(
+            [
+                jnp.concatenate([mid_w, empty], axis=1),
+                jnp.concatenate([empty, mid_w], axis=1),
+            ],
+            axis=0,
+        )
+
     def matrix(layer, m):
         return w_ref[layer, m]
 
@@ -225,25 +237,31 @@
             copy.wait_recv()
         far = dot(state_tab[layer].reshape(576, 128), matrix(layer, FAR)).astype(BF16)
         far_tab[...] = far.reshape(6, 6, 16, 128)
-        mid_w = matrix(layer, MID)
         mid_b = b_ref[layer, 1:2, :]
 
         def row(x, _):
-            for y in range(4):
-                c = x * 4 + y
+            cells_here = [x * 4 + y for y in range(4)]
+            fetched = []
+            for y, c in enumerate(cells_here):
                 block = far_tab[pl.ds(x, 3), y : y + 3].reshape(144, 128)
                 block = jnp.concatenate([block, jnp.zeros((112, 128), BF16)], axis=0)
-                fetched = dot(pick[c], block)
+                fetched.append(dot(pick[c], block))
+            firsts = []
+            for y, c in enumerate(cells_here):
                 base = near[pl.ds(pl.multiple_of(c * 16, 16), 16), :]
-                pre_one = (fetched.reshape(16, 16, 128) + base[None]).reshape(256, 128)
+                pre_one = (fetched[y].reshape(16, 16, 128) + base[None]).reshape(256, 128)
                 value, slope = silu_parts(pre_one)
                 first = value.astype(BF16)
                 g_one[layer, c] = slope.astype(BF16)
                 first_t[layer, c] = first.T
-                pre_two = dot(first, mid_w) + mid_b
+                firsts.append(jnp.concatenate([first[:128], first[128:]], axis=1))
+            seconds = [dot(first, mid_pair[layer]) for first in firsts]
+            for y, c in enumerate(cells_here):
+                pre_two = jnp.concatenate([seconds[y][:, :128], seconds[y][:, 128:]], axis=0) + mid_b
                 value, slope = silu_parts(pre_two)
-                g_two[layer, c] = (slope * valid_b[c].astype(F32)).astype(BF16)
-                total = dot(group[c], value.astype(BF16))
+                flags = valid_b[c].astype(F32)
+                g_two[layer, c] = (slope * flags).astype(BF16)
+                total = jnp.sum((value * flags).reshape(16, 16, 128), axis=0)
                 pooled[layer, pl.ds(pl.multiple_of(c * 16, 16), 16), :] = total.astype(BF16)
             return 0
 
@@ -277,23 +295,38 @@
         return d_pre_b, d_msg, jnp.sum(d_pre, axis=0, keepdims=True)
 
     def edges_back(layer):
-        mid_w = matrix(layer, MID)
         far_acc[...] = jnp.zeros((6, 6, 16, 128), F32)
         mid_acc[...] = jnp.zeros((128, 128), F32)
 
         def row(x, mid_b_sum):
-            for y in range(4):
-                c = x * 4 + y
+            cells_here = [x * 4 + y for y in range(4)]
+            twos = []
+            for c in cells_here:
                 rows = pl.ds(pl.multiple_of(c * 16, 16), 16)
                 upper = d_pool[rows, :].astype(F32)
                 d_two = g_two[layer, c].astype(F32).reshape(16, 16, 128) * upper[None]
                 mid_b_sum = mid_b_sum + jnp.sum(d_two, axis=0)
-                d_two_b = d_two.reshape(256, 128).astype(BF16)
-                mid_acc[...] += dot(first_t[layer, c], d_two_b)
-                d_one = side_dot(d_two_b, mid_w) * g_one[layer, c].astype(F32)
+                twos.append(d_two.reshape(256, 128).astype(BF16))
+            outs = [
+                side_dot(jnp.concatenate([t[:128], t[128:]], axis=1), mid_pair[layer]) for t in twos
+            ]
+            ones = []
+            for y, c in enumerate(cells_here):
+                rows = pl.ds(pl.multiple_of(c * 16, 16), 16)
+                d_first = jnp.concatenate([outs[y][:, :128], outs[y][:, 128:]], axis=0)
+                d_one = d_first * g_one[layer, c].astype(F32)
                 d_near[rows, :] = jnp.sum(d_one.reshape(16, 16, 128), axis=0)
-                spill = dot(place[c], d_one.astype(BF16))
-                far_acc[pl.ds(x, 3), y : y + 3] += spill.reshape(3, 3, 16, 128)
+                ones.append(d_one.astype(BF16))
+            both = [
+                dot(
+                    jnp.concatenate([first_t[layer, c], place[c]], axis=0),
+                    jnp.concatenate([twos[y], ones[y]], axis=1),
+                )
+                for y, c in enumerate(cells_here)
+            ]
+            mid_acc[...] += sum(b[:128, :128] for b in both)
+            for y in range(4):
+                far_acc[pl.ds(x, 3), y : y + 3] += both[y][128:, 128:].reshape(3, 3, 16, 128)
             return mid_b_sum
 
         mid_b_sum = lax.fori_loop(0, 4, row, jnp.zeros((16, 128), F32))
@@ -531,6 +564,7 @@
             vmem((2, 6, 6, 16, 128), BF16),
             vmem((2, 8, 4, 16, 128), BF16),
             vmem((128, 128), F32),
+            vmem((2, 256, 256), BF16),
             vmem((ring, early, 128), BF16),
             vmem((ring, early, 128), BF16),
             vmem((depth, early, 128), BF16),

time: 72.9 us -> 66.2 us (0.908)
  Pallas kernels: 63.4 us -> 56.7 us
    pallas_call x1, Pallas kernels: 63.4 us -> 56.7 us  [shards(): pl.pallas_call(functools.partial(kernel, gx, gy), out_shape=(jax.ShapeDty...]
where the time goes in v2:
time: 66.2 us; the launch traced here: 65.9 us
  Pallas kernels  56.7 us (86%)
  local copies, waits for them, and re-layouts  7.53 us (11%)
  other arithmetic  1.02 us (2%)
    pallas_call x1, Pallas kernels, shards(): pl.pallas_call(functools.partial(kernel, gx, gy), out_shape=(jax.ShapeDty...  56.7 us
    unnamed x17, local copies, waits for them, and re-layouts  7.52 us

profile of v2, /device:TPU:1, one launch (start us, length us, event | category | flops | bytes accessed | tf_op | source)
XLA Modules:
  0.0 65.9 jit_solution(16182252177040331711)
XLA Ops:
  0.6 0.0 copy-start.6
  0.6 0.7 %copy-done.6 = f32[2,3,128]{2,0,1:T(2,128)S(1)} copy-done((f32[2,3,128]{2,0,1:T(2,128)S(1)}, f32[2,3,128]{2,0,1:T(2,128)}, u32[]{:S(2)}) %copy-start.6) | copy-done | bytes 3096
  1.3 0.0 copy-start
  1.3 1.0 %copy-done = s32[2,2,4,4,16,128]{5,4,3,2,1,0:T(8,128)S(1)} copy-done((s32[2,2,4,4,16,128]{5,4,3,2,1,0:T(8,128)S(1)}, s32[2,2,4,4,16,128]{5,4,3,2,1,0:T(8,128)}, u32[]{:S(2)}) %copy-start) | copy-done | bytes 524312
  2.4 0.0 copy-start.1
  2.4 1.0 %copy-done.1 = bf16[2,7,128,128]{3,2,1,0:T(8,128)(2,1)S(1)} copy-done((bf16[2,7,128,128]{3,2,1,0:T(8,128)(2,1)S(1)}, bf16[2,7,128,128]{3,2,1,0:T(8,128)(2,1)}, u32[]{:S(2)}) %copy-start.1) | copy-done | bytes 458776
  3.4 0.0 copy-start.2
  3.4 0.9 %copy-done.2 = s32[4,4,16,16]{3,2,1,0:T(8,128)S(1)} copy-done((s32[4,4,16,16]{3,2,1,0:T(8,128)S(1)}, s32[4,4,16,16]{3,2,1,0:T(8,128)}, u32[]{:S(2)}) %copy-start.2) | copy-done | bytes 16408
  4.3 0.0 copy-start.3
  4.3 0.9 %copy-done.3 = s32[4,4,16,16]{3,2,1,0:T(8,128)S(1)} copy-done((s32[4,4,16,16]{3,2,1,0:T(8,128)S(1)}, s32[4,4,16,16]{3,2,1,0:T(8,128)}, u32[]{:S(2)}) %copy-start.3) | copy-done | bytes 16408
  5.2 0.0 copy-start.4
  5.2 0.9 %copy-done.4 = f32[4,4,16,128]{3,2,1,0:T(8,128)S(1)} copy-done((f32[4,4,16,128]{3,2,1,0:T(8,128)S(1)}, f32[4,4,16,128]{3,2,1,0:T(8,128)}, u32[]{:S(2)}) %copy-start.4) | copy-done | bytes 131096
  6.1 0.0 copy-start.5
  6.1 0.8 %copy-done.5 = bf16[4,4,16,128]{3,2,1,0:T(8,128)(2,1)S(1)} copy-done((bf16[4,4,16,128]{3,2,1,0:T(8,128)(2,1)S(1)}, bf16[4,4,16,128]{3,2,1,0:T(8,128)(2,1)}, u32[]{:S(2)}) %copy-start.5) | copy-done | bytes 65560
  6.9 56.7 %evolver.1 = (f32[256,128]{1,0:T(8,128)S(1)}, bf16[2,7,128,128]{3,2,1,0:T(8,128)(2,1)S(1)}, f32[8,128]{1,0:T(8,128)S(1)}) custom-call(bf16[4,4,16,128]{3,2,1,0:T(8,128)(2,1)S(1)} %copy-done.5, s32[16,16,16]{2,1,0:T(8,128)S(1)} %bitcast.7, s32[16,16,16]{2,1,0:T(8,128)S(1)} %bitcast.8, s32[4,256,128]{2,1,0:T(8,128)S(1)} %bitcast.5, ...), custom_call_target="tpu_custom_call" | custom-call | tf_op jit(solution)/shard_map/evolver/pallas_call | solution.py:584
  63.6 0.6 copy.13
  64.2 1.0 %convert_multiply_fusion = f32[2,7,128,128]{3,2,1,0:T(8,128)} fusion(bf16[2,7,128,128]{3,2,1,0:T(8,128)(2,1)S(1)} %get-tuple-element.7), kind=kLoop, calls=%fused_computation | loop fusion | flops 458752 | bytes 1376256 | tf_op jit(solution)/shard_map/mul | solution.py:609
  65.2 0.7 copy.15
  (3 shorter events, 0.0 us)
Async XLA Ops:
  0.6 0.7 %copy-start.6 = (f32[2,3,128]{2,0,1:T(2,128)S(1)}, f32[2,3,128]{2,0,1:T(2,128)}, u32[]{:S(2)}) copy-start(f32[2,3,128]{2,0,1:T(2,128)} %param.12) | copy-start | bytes 9220
  1.3 1.0 %copy-start = (s32[2,2,4,4,16,128]{5,4,3,2,1,0:T(8,128)S(1)}, s32[2,2,4,4,16,128]{5,4,3,2,1,0:T(8,128)}, u32[]{:S(2)}) copy-start(s32[2,2,4,4,16,128]{5,4,3,2,1,0:T(8,128)} %param.10) | copy-start | bytes 1572868
  2.4 1.0 %copy-start.1 = (bf16[2,7,128,128]{3,2,1,0:T(8,128)(2,1)S(1)}, bf16[2,7,128,128]{3,2,1,0:T(8,128)(2,1)}, u32[]{:S(2)}) copy-start(bf16[2,7,128,128]{3,2,1,0:T(8,128)(2,1)} %w_ref.1) | copy-start | bytes 1376260
  3.4 0.9 %copy-start.2 = (s32[4,4,16,16]{3,2,1,0:T(8,128)S(1)}, s32[4,4,16,16]{3,2,1,0:T(8,128)}, u32[]{:S(2)}) copy-start(s32[4,4,16,16]{3,2,1,0:T(8,128)} %param.8) | copy-start | bytes 49156
  4.3 0.9 %copy-start.3 = (s32[4,4,16,16]{3,2,1,0:T(8,128)S(1)}, s32[4,4,16,16]{3,2,1,0:T(8,128)}, u32[]{:S(2)}) copy-start(s32[4,4,16,16]{3,2,1,0:T(8,128)} %param.9) | copy-start | bytes 49156
  5.2 0.9 %copy-start.4 = (f32[4,4,16,128]{3,2,1,0:T(8,128)S(1)}, f32[4,4,16,128]{3,2,1,0:T(8,128)}, u32[]{:S(2)}) copy-start(f32[4,4,16,128]{3,2,1,0:T(8,128)} %param.13) | copy-start | bytes 393220
  6.1 0.8 %copy-start.5 = (bf16[4,4,16,128]{3,2,1,0:T(8,128)(2,1)S(1)}, bf16[4,4,16,128]{3,2,1,0:T(8,128)(2,1)}, u32[]{:S(2)}) copy-start(bf16[4,4,16,128]{3,2,1,0:T(8,128)(2,1)} %part_ref.1) | copy-start | bytes 196612

commit v3 on v1

v3 whole, which is shorter than its diff:
```python
import functools

import jax
import jax.experimental.pallas as pl
import jax.experimental.pallas.tpu as pltpu
import jax.numpy as jnp
from jax import lax
from jax.sharding import PartitionSpec as P

MESH = pl.DeviceIdType.MESH
BF16, F32 = jnp.bfloat16, jnp.float32
keep_scale = 10.0 / 9.0
VMEM_BYTES = 60 * 2**20

Y_HI = 2
NEAR, FAR, SELF, MSG, MID, POOL, OUT = range(7)
TOP = [(1, m) for m in range(7)]
NODE = [(0, OUT), (0, SELF), (0, MSG), (0, POOL)]
EDGE = [(0, NEAR), (0, FAR), (0, MID)]
GROUPS = [TOP, NODE, EDGE]
TILES = [64, 32, 32]
BIAS_TILE = 24
ROUTES = [(1, 0), (-1, 0), (0, 1), (0, -1), (1, 1), (1, -1), (-1, 1), (-1, -1)]
BORDER = [[0, 1, 2, 3], [12, 13, 14, 15], [4, 8, 7, 11]]
INSIDE = [[5, 6, 9, 10]]


def dot(a, b):
    return jnp.dot(a, b, preferred_element_type=F32)


def side_dot(a, b):
    return lax.dot_general(a, b, (((1,), (1,)), ((), ())), preferred_element_type=F32)


def back_dot(a, b):
    return lax.dot_general(a, b, (((0,), (0,)), ((), ())), preferred_element_type=F32)


def silu_parts(v):
    sig = 0.5 * jnp.tanh(0.5 * v) + 0.5
    value = v * sig
    return value, sig + value * (1.0 - sig)


def ones_where(mask):
    return jnp.where(mask, 1.0, 0.0)


def flat(fours):
    return [c for four in fours for c in four]


def rows_of(ref, cells):
    return jnp.concatenate([ref[c * 16 : (c + 1) * 16, :] for c in cells], axis=0)


def set_rows(ref, cells, value):
    for n, c in enumerate(cells):
        ref[c * 16 : (c + 1) * 16, :] = value[n * 16 : (n + 1) * 16]


def halves_side_by_side(a):
    return jnp.concatenate([a[:128], a[128:]], axis=1)


def halves_stacked(a):
    return jnp.concatenate([a[:, :128], a[:, 128:]], axis=0)


def kernel(
    gx,
    gy,
    norm_scale,
    part_hbm,
    code_hbm,
    valid_hbm,
    drop_hbm,
    w_hbm,
    b_hbm,
    cot_hbm,
    pgrad_hbm,
    wgrad_hbm,
    bgrad_hbm,
    pgrad_ref,
    wgrad_ref,
    bgrad_ref,
    code_ref,
    valid_ref,
    drop_ref,
    w_ref,
    b_ref,
    cot_ref,
    state_tab,
    far_tab,
    pick,
    place,
    valid_b,
    code_rows,
    near,
    g_one,
    g_two,
    first_t,
    pooled,
    message,
    hidden,
    g_node,
    up_b_ref,
    upstream,
    d_pre_ref,
    d_msg_ref,
    d_pool,
    d_near,
    far_acc,
    far_send,
    far_recv,
    mid_acc,
    mid_pair,
    *rest,
):
    groups = [rest[n * 6 : n * 6 + 6] for n in range(3)]
    (
        in_sem,
        out_sem,
        halo_send_sem,
        halo_recv_sem,
        back_send_sem,
        back_recv_sem,
        red_send_sem,
        red_recv_sem,
    ) = rest[18:]
    me_x = lax.axis_index("gx")
    me_y = lax.axis_index("gy")
    depth = gy // Y_HI
    plane = gx * Y_HI // 2
    me_z = lax.rem(me_y, depth)
    core = lax.rem(me_x, 2)
    me_p = (me_x // 4) * 4 + (me_y // depth) * 2 + lax.rem(me_x // 2, 2)

    def plane_device(p):
        return (
            (p // 4) * 4 + lax.rem(p, 2) * 2 + core,
            lax.rem(p // 2, 2) * depth + me_z,
        )

    def z_device(z):
        return (me_x, me_y - me_z + z)

    partner = (me_x + 1 - 2 * core, me_y)

    def neighbour(dx, dy):
        return (lax.rem(me_x + dx + gx, gx), lax.rem(me_y + dy + gy, gy))

    barrier = pltpu.get_barrier_semaphore()

    def greet(device):
        pl.semaphore_signal(barrier, inc=1, device_id=device, device_id_type=MESH)

    for dx, dy in ROUTES:
        greet(neighbour(dx, dy))

    def greet_plane(d, _):
        greet(plane_device(lax.rem(me_p + d, plane)))
        return 0

    def greet_z(d, _):
        greet(z_device(lax.rem(me_z + d, depth)))
        return 0

    lax.fori_loop(1, plane, greet_plane, 0)
    lax.fori_loop(1, depth, greet_z, 0)

    loads = [
        pltpu.make_async_copy(source, target, in_sem.at[n])
        for n, (source, target) in enumerate(
            [
                (part_hbm, state_tab.at[0, pl.ds(1, 4), pl.ds(1, 4)]),
                (code_hbm, code_ref),
                (valid_hbm, valid_ref),
                (w_hbm, w_ref),
                (b_hbm, b_ref),
                (drop_hbm, drop_ref),
                (cot_hbm, cot_ref),
            ]
        )
    ]
    for load in loads:
        load.start()

    def part(step, edge):
        return pl.ds(1, 4) if step == 0 else pl.ds(edge[0] if step > 0 else edge[1], 1)

    def halo_copies(layer):
        copies = []
        for n, (dx, dy) in enumerate(ROUTES):
            tab = state_tab.at[layer]
            copies.append(
                pltpu.make_async_remote_copy(
                    src_ref=tab.at[part(dx, (4, 1)), part(dy, (4, 1))],
                    dst_ref=tab.at[part(dx, (0, 5)), part(dy, (0, 5))],
                    send_sem=halo_send_sem.at[layer, n],
                    recv_sem=halo_recv_sem.at[layer, n],
                    device_id=neighbour(dx, dy),
                    device_id_type=MESH,
                )
            )
        return copies

    def back_copies(layer):
        copies = []
        for n, (dx, dy) in enumerate(ROUTES):
            x = pl.ds(1, 4) if dx == 0 else (5 if dx > 0 else 0)
            y = pl.ds(1, 4) if dy == 0 else (5 if dy > 0 else 0)
            target = far_recv.at[layer, n]
            copies.append(
                pltpu.make_async_remote_copy(
                    src_ref=far_send.at[layer, x, y],
                    dst_ref=target.at[0] if dx and dy else target,
                    send_sem=back_send_sem.at[layer, n],
                    recv_sem=back_recv_sem.at[layer, n],
                    device_id=neighbour(dx, dy),
                    device_id_type=MESH,
                )
            )
        return copies

    halos = [halo_copies(layer) for layer in range(2)]
    backs = [back_copies(layer) for layer in range(2)]

    spread = ones_where(
        lax.broadcasted_iota(jnp.int32, (16, 256), 1) // 16
        == lax.broadcasted_iota(jnp.int32, (16, 256), 0)
    ).astype(BF16)
    own = ones_where(
        lax.rem(lax.broadcasted_iota(jnp.int32, (256, 256), 0), 16)
        == lax.rem(lax.broadcasted_iota(jnp.int32, (256, 256), 1), 16)
    )
    gather_cell = ones_where(
        lax.broadcasted_iota(jnp.int32, (16, 256), 1) // 16
        == lax.broadcasted_iota(jnp.int32, (16, 256), 0)
    ).astype(BF16)
    loads[0].wait()
    loads[1].wait()
    loads[2].wait()
    codes = code_ref[...].reshape(256, 16).astype(F32).astype(BF16)
    code_rows[...] = dot(gather_cell, (dot(codes, spread) * own).astype(BF16))

    pl.semaphore_wait(barrier, plane - 1 + depth - 1 + len(ROUTES))
    for copy in halos[0]:
        copy.start()

    slot_rows = lax.broadcasted_iota(jnp.int32, (144, 256), 0).astype(F32)
    slot_lanes = lax.broadcasted_iota(jnp.int32, (16, 256), 1).astype(F32)

    def prepare(c, _):
        row = code_rows[pl.ds(c, 1), :]
        place[c] = ones_where(slot_rows == row).astype(BF16)
        code = code_ref[c].astype(F32)
        flag = valid_ref[c].astype(F32)
        for k in range(16):
            rows = slice(k * 16, (k + 1) * 16)
            column = jnp.broadcast_to(code[:, k : k + 1], (16, 256))
            pick[c, rows, :] = ones_where(column == slot_lanes).astype(BF16)
            valid_b[c, rows, :] = jnp.broadcast_to(flag[:, k : k + 1], (16, 128)).astype(BF16)
        return 0

    lax.fori_loop(0, 16, prepare, 0)
    for load in loads[3:]:
        load.wait()
    empty = jnp.zeros((128, 128), BF16)
    for layer in range(2):
        mid_w = w_ref[layer, MID]
        mid_pair[layer] = jnp.concatenate(
            [
                jnp.concatenate([mid_w, empty], axis=1),
                jnp.concatenate([empty, mid_w], axis=1),
            ],
            axis=0,
        )

    def matrix(layer, m):
        return w_ref[layer, m]

    def bias(layer, m):
        return b_ref[m, layer : layer + 1, :]

    def state_of(layer, cells):
        return jnp.concatenate(
            [state_tab[layer, c // 4 + 1, c % 4 + 1] for c in cells], axis=0
        )

    def inner_state(layer):
        return state_tab[layer, 1:5, 1:5].reshape(256, 128)

    def padded_state(layer):
        return state_tab[layer].reshape(576, 128)

    def kept(layer, which, cells, scale):
        return rows_of(drop_ref.at[2 * layer + which], cells).astype(F32) * scale

    def own_projections(layer):
        state = inner_state(layer)
        near[...] = dot(state, matrix(layer, NEAR)) + bias(layer, 0)
        far = dot(state, matrix(layer, FAR)).astype(BF16)
        far_tab[1:5, 1:5] = far.reshape(4, 4, 16, 128)

    def halo_projections(layer):
        for copy in halos[layer]:
            copy.wait_recv()
        pieces = [
            state_tab[layer, 0].reshape(96, 128),
            state_tab[layer, 5].reshape(96, 128),
            state_tab[layer, 1:5, 0].reshape(64, 128),
            state_tab[layer, 1:5, 5].reshape(64, 128),
        ]
        far = dot(jnp.concatenate(pieces, axis=0), matrix(layer, FAR)).astype(BF16)
        far_tab[0] = far[0:96].reshape(6, 16, 128)
        far_tab[5] = far[96:192].reshape(6, 16, 128)
        far_tab[1:5, 0] = far[192:256].reshape(4, 16, 128)
        far_tab[1:5, 5] = far[256:320].reshape(4, 16, 128)

    def edges_forward(layer, cells):
        fetched = []
        for c in cells:
            x, y = c // 4, c % 4
            block = far_tab[x : x + 3, y : y + 3].reshape(144, 128)
            block = jnp.concatenate([block, jnp.zeros((112, 128), BF16)], axis=0)
            fetched.append(dot(pick[c], block))
        firsts = []
        for n, c in enumerate(cells):
            base = near[c * 16 : (c + 1) * 16, :]
            pre_one = (fetched[n].reshape(16, 16, 128) + base[None]).reshape(256, 128)
            value, slope = silu_parts(pre_one)
            first = value.astype(BF16)
            g_one[layer, c] = slope.astype(BF16)
            first_t[layer, c] = first.T
            firsts.append(halves_side_by_side(first))
        seconds = [dot(first, mid_pair[layer]) for first in firsts]
        for n, c in enumerate(cells):
            value, slope = silu_parts(halves_stacked(seconds[n]) + bias(layer, 1))
            flags = valid_b[c].astype(F32)
            g_two[layer, c] = (slope * flags).astype(BF16)
            total = jnp.sum((value * flags).reshape(16, 16, 128), axis=0)
            pooled[layer, c * 16 : (c + 1) * 16, :] = total.astype(BF16)

    def nodes_forward(layer, cells):
        state = state_of(layer, cells)
        keep_msg = kept(layer, 0, cells, keep_scale / 16)
        keep_node = kept(layer, 1, cells, keep_scale)
        total = rows_of(pooled.at[layer], cells)
        msg = (dot(total, matrix(layer, POOL)) * keep_msg).astype(BF16)
        set_rows(message.at[layer], cells, msg)
        node_pre = dot(state, matrix(layer, SELF)) + dot(msg, matrix(layer, MSG)) + bias(layer, 2)
        value, slope = silu_parts(node_pre)
        node_hidden = (value * keep_node).astype(BF16)
        set_rows(hidden.at[layer], cells, node_hidden)
        set_rows(g_node.at[layer], cells, slope * keep_node)
        if layer == 0:
            after = (state.astype(F32) + dot(node_hidden, matrix(0, OUT))).astype(BF16)
            for n, c in enumerate(cells):
                state_tab[1, c // 4 + 1, c % 4 + 1] = after[n * 16 : (n + 1) * 16]

    own_projections(0)
    halo_projections(0)
    for four in BORDER:
        edges_forward(0, four)
    nodes_forward(0, flat(BORDER))
    for copy in halos[1]:
        copy.start()
    for four in INSIDE:
        edges_forward(0, four)
    nodes_forward(0, flat(INSIDE))
    own_projections(1)
    for four in INSIDE:
        edges_forward(1, four)
    nodes_forward(1, flat(INSIDE))
    halo_projections(1)
    for four in BORDER:
        edges_forward(1, four)
    nodes_forward(1, flat(BORDER))

    def node_back(layer, cells):
        up_b = rows_of(upstream, cells).astype(BF16)
        set_rows(up_b_ref, cells, up_b)
        d_pre = side_dot(up_b, matrix(layer, OUT)) * rows_of(g_node.at[layer], cells)
        d_pre_b = d_pre.astype(BF16)
        set_rows(d_pre_ref, cells, d_pre_b)
        keep_msg = kept(layer, 0, cells, keep_scale / 16)
        d_msg = (side_dot(d_pre_b, matrix(layer, MSG)) * keep_msg).astype(BF16)
        set_rows(d_msg_ref, cells, d_msg)
        set_rows(d_pool, cells, side_dot(d_msg, matrix(layer, POOL)).astype(BF16))
        return jnp.sum(d_pre, axis=0, keepdims=True)

    def edges_back(layer, cells, mid_b_sum):
        twos = []
        for c in cells:
            upper = d_pool[c * 16 : (c + 1) * 16, :].astype(F32)
            d_two = g_two[layer, c].astype(F32).reshape(16, 16, 128) * upper[None]
            mid_b_sum = mid_b_sum + jnp.sum(d_two, axis=0)
            twos.append(d_two.reshape(256, 128).astype(BF16))
        outs = [side_dot(halves_side_by_side(two), mid_pair[layer]) for two in twos]
        ones = []
        for n, c in enumerate(cells):
            d_one = halves_stacked(outs[n]) * g_one[layer, c].astype(F32)
            d_near[c * 16 : (c + 1) * 16, :] = jnp.sum(d_one.reshape(16, 16, 128), axis=0)
            ones.append(d_one.astype(BF16))
        both = [
            dot(
                jnp.concatenate([first_t[layer, c], place[c]], axis=0),
                jnp.concatenate([twos[n], ones[n]], axis=1),
            )
            for n, c in enumerate(cells)
        ]
        mid_acc[...] += sum(b[:128, :128] for b in both)
        for n, c in enumerate(cells):
            x, y = c // 4, c % 4
            far_acc[x : x + 3, y : y + 3] += both[n][128:, 128:].reshape(3, 3, 16, 128)
        return mid_b_sum

    def clear_sums():
        far_acc[...] = jnp.zeros((6, 6, 16, 128), F32)
        mid_acc[...] = jnp.zeros((128, 128), F32)

    def send_far(layer):
        far_send[layer, 0] = far_acc[0].astype(BF16)
        far_send[layer, 5] = far_acc[5].astype(BF16)
        far_send[layer, 1:5, 0] = far_acc[1:5, 0].astype(BF16)
        far_send[layer, 1:5, 5] = far_acc[1:5, 5].astype(BF16)
        for copy in backs[layer]:
            copy.start()

    def add_arrivals(layer):
        for n, (dx, dy) in enumerate(ROUTES):
            backs[layer][n].wait_recv()
            x = pl.ds(1, 4) if dx == 0 else pl.ds(1 if dx > 0 else 4, 1)
            y = pl.ds(1, 4) if dy == 0 else pl.ds(1 if dy > 0 else 4, 1)
            block = far_recv[layer, n].astype(F32)
            if dx and dy:
                far_acc[x, y] += block[0:1][None]
            elif dx:
                far_acc[x, y] += block[None]
            else:
                far_acc[x, y] += block[:, None]

    def far_rows(cells):
        return jnp.concatenate(
            [far_acc[c // 4 + 1, c % 4 + 1] for c in cells], axis=0
        ).astype(BF16)

    def new_upstream(layer, cells):
        return (
            rows_of(upstream, cells)
            + side_dot(rows_of(d_pre_ref, cells), matrix(layer, SELF))
            + side_dot(rows_of(d_near, cells).astype(BF16), matrix(layer, NEAR))
            + side_dot(far_rows(cells), matrix(layer, FAR))
        )

    def spans(n, index):
        rows = groups[n][0].shape[2]
        found = []
        done = 0
        while done < 128:
            chunk, offset = divmod(index * 128 + done, rows)
            count = min(rows - offset, 128 - done)
            found.append((done, count, chunk // plane, chunk % plane, offset))
            done += count
        return found

    def put(layer, m, value):
        value = value.astype(BF16)
        for n in range(3):
            if (layer, m) in GROUPS[n]:
                stage = groups[n][0]
                for done, count, half, p, offset in spans(n, GROUPS[n].index((layer, m))):
                    stage[half, p, offset : offset + count, :] = value[done : done + count]

    def take(n):
        gathered = groups[n][5]
        for index, (layer, m) in enumerate(GROUPS[n]):
            for done, count, half, p, offset in spans(n, index):
                piece = gathered[half, p, offset : offset + count, :]
                wgrad_ref[layer, m, done : done + count, :] = piece.astype(F32) * norm_scale

    def clear_rest(n, used):
        stage = groups[n][0]
        rows = stage.shape[2]
        while used < TILES[n] * 16:
            chunk, offset = divmod(used, rows)
            stage[chunk // plane, chunk % plane, offset:rows, :] = jnp.zeros(
                (rows - offset, 128), BF16
            )
            used += rows - offset

    def edge_grads(layer):
        put(layer, MID, mid_acc[...])
        near_b = d_near[...].astype(BF16)
        put(layer, NEAR, back_dot(inner_state(layer), near_b))
        far_b = far_acc[...].astype(BF16).reshape(576, 128)
        put(layer, FAR, back_dot(padded_state(layer), far_b))
        return jnp.sum(d_near[...], axis=0, keepdims=True)

    def node_grads(layer):
        put(layer, OUT, back_dot(hidden[layer], up_b_ref[...]))
        put(layer, SELF, back_dot(inner_state(layer), d_pre_ref[...]))
        put(layer, MSG, back_dot(message[layer], d_pre_ref[...]))
        put(layer, POOL, back_dot(pooled[layer], d_msg_ref[...]))

    bias_rows = TILES[2] // (2 * plane) * 16
    bias_chunk, bias_offset = divmod(BIAS_TILE * 16, bias_rows)
    bias_half, bias_p = divmod(bias_chunk, plane)
    bias_here = slice(bias_offset, bias_offset + 16)

    def split_again(tile):
        both = tile[0:8] + tile[8:16]
        high = both.astype(BF16).astype(F32)
        return jnp.concatenate([high, both - high], axis=0).astype(BF16)

    def remote(source, target, sem, device):
        return pltpu.make_async_remote_copy(
            src_ref=source,
            dst_ref=target,
            send_sem=red_send_sem.at[sem],
            recv_sem=red_recv_sem.at[sem],
            device_id=device,
            device_id_type=MESH,
        )

    def wait_all(sems, sem, buffer, count):
        view = buffer.at[pl.ds(0, count)]
        pltpu.make_async_copy(view, view, sems.at[sem]).wait()

    def fold(buffer, count):
        total = buffer[0].astype(F32)
        for n in range(1, count):
            total = total + buffer[n].astype(F32)
        return total

    def core_copy(n):
        return remote(groups[n][0].at[1 - core], groups[n][1], 5 * n, partner)

    def share_copy(n):
        return remote(groups[n][5].at[core], groups[n][5].at[core], 5 * n + 4, partner)

    def over_core(n):
        core_copy(n).start()

    def over_plane(n):
        stage, arrived, added, slots, across, gathered = groups[n]
        core_copy(n).wait_recv()
        total = stage[core].astype(F32) + arrived[...].astype(F32)
        added[...] = total.astype(BF16)
        if n == 2:
            tile = total[bias_p, bias_here]
            added[bias_p, bias_here] = jnp.where(
                core == bias_half, split_again(tile), tile.astype(BF16)
            )

        def body(d, _):
            p = lax.rem(me_p + d, plane)
            remote(added.at[p], slots.at[me_p], 5 * n + 1, plane_device(p)).start()
            return 0

        lax.fori_loop(1, plane, body, 0)
        slots[me_p] = added[me_p]

    def rounded(n, total):
        plain = total.astype(BF16)
        if n < 2:
            return plain
        mine = jnp.logical_and(core == bias_half, me_p == bias_p)
        pieces = [
            plain[:bias_offset],
            jnp.where(mine, split_again(total[bias_here]), plain[bias_here]),
            plain[bias_offset + 16 :],
        ]
        return jnp.concatenate([p for p in pieces if p.shape[0]], axis=0)

    def over_z(n):
        stage, arrived, added, slots, across, gathered = groups[n]
        wait_all(red_recv_sem, 5 * n + 1, slots, plane - 1)
        across[me_z] = rounded(n, fold(slots, plane))

        def body(d, _):
            z = lax.rem(me_z + d, depth)
            remote(across.at[me_z], across.at[me_z], 5 * n + 2, z_device(z)).start()
            return 0

        lax.fori_loop(1, depth, body, 0)

    def back_over_plane(n):
        stage, arrived, added, slots, across, gathered = groups[n]
        wait_all(red_recv_sem, 5 * n + 2, across, depth - 1)
        gathered[core, me_p] = rounded(n, fold(across, depth))

        def body(d, _):
            p = lax.rem(me_p + d, plane)
            here = gathered.at[core, me_p]
            remote(here, here, 5 * n + 3, plane_device(p)).start()
            return 0

        lax.fori_loop(1, plane, body, 0)

    def back_over_core(n):
        gathered = groups[n][5]
        wait_all(red_recv_sem, 5 * n + 3, gathered.at[core], plane - 1)
        share_copy(n).start()

    def arrived_whole(n):
        pltpu.make_async_copy(
            groups[n][5].at[1 - core], groups[n][5].at[1 - core], red_recv_sem.at[5 * n + 4]
        ).wait()

    runs = [(1, 0, 7), (0, SELF, 2), (0, POOL, 2), (0, NEAR, 2), (0, MID, 1)]
    outs = [
        pltpu.make_async_copy(
            wgrad_ref.at[layer, pl.ds(m, count)],
            wgrad_hbm.at[layer, pl.ds(m, count)],
            out_sem.at[n],
        )
        for n, (layer, m, count) in enumerate(runs)
    ]
    outs.append(pltpu.make_async_copy(pgrad_ref, pgrad_hbm, out_sem.at[5]))
    outs.append(pltpu.make_async_copy(bgrad_ref, bgrad_hbm, out_sem.at[6]))

    no_sum = jnp.zeros((16, 128), F32)

    upstream[...] = cot_ref[...]
    node_b1 = node_back(1, list(range(16)))
    clear_sums()
    mid_b1 = no_sum
    for four in BORDER:
        mid_b1 = edges_back(1, four, mid_b1)
    send_far(1)
    for four in INSIDE:
        mid_b1 = edges_back(1, four, mid_b1)
    edge_b1 = edge_grads(1)
    node_grads(1)
    clear_rest(0, len(TOP) * 128)
    over_core(0)

    set_rows(upstream, flat(INSIDE), new_upstream(1, flat(INSIDE)))
    node_b0 = node_back(0, flat(INSIDE))
    over_plane(0)
    add_arrivals(1)
    set_rows(upstream, flat(BORDER), new_upstream(1, flat(BORDER)))
    clear_sums()
    node_b0 = node_b0 + node_back(0, flat(BORDER))
    node_grads(0)
    over_core(1)
    mid_b0 = no_sum
    for four in BORDER:
        mid_b0 = edges_back(0, four, mid_b0)
    send_far(0)
    over_plane(1)
    over_z(0)
    for four in INSIDE:
        mid_b0 = edges_back(0, four, mid_b0)
    edge_b0 = edge_grads(0)
    column = [jnp.sum(v, axis=0, keepdims=True) for v in (mid_b0, mid_b1)]
    sums = jnp.concatenate(
        [edge_b0, edge_b1, column[0], column[1], node_b0, node_b1, jnp.zeros((2, 128), F32)],
        axis=0,
    )
    high = sums.astype(BF16).astype(F32)
    groups[2][0][bias_half, bias_p, bias_here, :] = jnp.concatenate(
        [high, sums - high], axis=0
    ).astype(BF16)
    clear_rest(2, (BIAS_TILE + 1) * 16)
    over_core(2)
    back_over_plane(0)
    over_plane(2)
    over_z(1)
    add_arrivals(0)
    pgrad_ref[...] = new_upstream(0, list(range(16)))
    outs[5].start()
    over_z(2)
    back_over_plane(1)
    back_over_core(0)
    back_over_plane(2)
    arrived_whole(0)
    take(0)
    outs[0].start()
    back_over_core(1)
    arrived_whole(1)
    take(1)
    outs[1].start()
    outs[2].start()
    back_over_core(2)
    arrived_whole(2)
    take(2)
    outs[3].start()
    outs[4].start()
    pair = groups[2][5][bias_half, bias_p, bias_here, :].astype(F32)
    bias_total = (pair[0:8] + pair[8:16]) * norm_scale
    for m in range(3):
        bgrad_ref[m] = bias_total[2 * m : 2 * m + 2]
    outs[6].start()

    for layer in range(2):
        for copy in halos[layer] + backs[layer]:
            copy.wait_send()
    for n in range(3):
        stage, arrived, added, slots, across, gathered = groups[n]
        core_copy(n).wait_send()
        wait_all(red_send_sem, 5 * n + 1, slots, plane - 1)
        wait_all(red_send_sem, 5 * n + 2, across, depth - 1)
        wait_all(red_send_sem, 5 * n + 3, gathered.at[core], plane - 1)
        share_copy(n).wait_send()
    for out in outs:
        out.wait()


def write_out(pgrad, wgrad, bgrad, pgrad_out, wgrad_out, bgrad_out, pbuf, wbuf, bbuf, in_sems, out_sems):
    routes = [(pgrad, pbuf, pgrad_out), (bgrad, bbuf, bgrad_out)]
    for layer in range(2):
        for m, count in ((0, 2), (2, 2), (4, 3)):
            part = (layer, pl.ds(m, count))
            routes.append((wgrad.at[part], wbuf.at[part], wgrad_out.at[part]))
    reads = [pltpu.make_async_copy(a, b, in_sems.at[n]) for n, (a, b, _) in enumerate(routes)]
    writes = [pltpu.make_async_copy(b, c, out_sems.at[n]) for n, (_, b, c) in enumerate(routes)]
    for read in reads:
        read.start()
    for read, write in zip(reads, writes):
        read.wait()
        write.start()
    for write in writes:
        write.wait()


def solution(mesh):
    gx, gy = mesh.shape["gx"], mesh.shape["gy"]
    plane, depth = gx * Y_HI // 2, gy // Y_HI
    norm_scale = 1.0 / (gx * gy * 256) ** 0.5
    vmem = pltpu.VMEM

    def group_buffers(tiles):
        rows = tiles // (2 * plane) * 16
        return [
            vmem((2, plane, rows, 128), BF16),
            vmem((plane, rows, 128), BF16),
            vmem((plane, rows, 128), BF16),
            vmem((plane, rows, 128), BF16),
            vmem((depth, rows, 128), BF16),
            vmem((2, plane, rows, 128), BF16),
        ]

    def shards(particles, neighbours, edge_valid, dropout_keep, weights, biases, cotangent):
        scratch = [
            vmem((256, 128), F32),
            vmem((2, 7, 128, 128), F32),
            vmem((3, 2, 128), F32),
            vmem((16, 16, 16), jnp.int32),
            vmem((16, 16, 16), jnp.int32),
            vmem((4, 256, 128), jnp.int32),
            vmem((2, 7, 128, 128), BF16),
            vmem((3, 2, 128), F32),
            vmem((256, 128), F32),
            vmem((2, 6, 6, 16, 128), BF16),
            vmem((6, 6, 16, 128), BF16),
            vmem((16, 256, 256), BF16),
            vmem((16, 144, 256), BF16),
            vmem((16, 256, 128), BF16),
            vmem((16, 256), F32),
            vmem((256, 128), F32),
            vmem((2, 16, 256, 128), BF16),
            vmem((2, 16, 256, 128), BF16),
            vmem((2, 16, 128, 256), BF16),
            vmem((2, 256, 128), BF16),
            vmem((2, 256, 128), BF16),
            vmem((2, 256, 128), BF16),
            vmem((2, 256, 128), F32),
            vmem((256, 128), BF16),
            vmem((256, 128), F32),
            vmem((256, 128), BF16),
            vmem((256, 128), BF16),
            vmem((256, 128), BF16),
            vmem((256, 128), F32),
            vmem((6, 6, 16, 128), F32),
            vmem((2, 6, 6, 16, 128), BF16),
            vmem((2, 8, 4, 16, 128), BF16),
            vmem((128, 128), F32),
            vmem((2, 256, 256), BF16),
        ]
        for tiles in TILES:
            scratch += group_buffers(tiles)
        scratch += [
            pltpu.SemaphoreType.DMA((7,)),
            pltpu.SemaphoreType.DMA((7,)),
            pltpu.SemaphoreType.DMA((2, 8)),
            pltpu.SemaphoreType.DMA((2, 8)),
            pltpu.SemaphoreType.DMA((2, 8)),
            pltpu.SemaphoreType.DMA((2, 8)),
            pltpu.SemaphoreType.DMA((15,)),
            pltpu.SemaphoreType.DMA((15,)),
        ]
        far_off = pl.BlockSpec(memory_space=pl.ANY)
        shapes = (
            jax.ShapeDtypeStruct((256, 128), F32),
            jax.ShapeDtypeStruct((2, 7, 128, 128), F32),
            jax.ShapeDtypeStruct((3, 2, 128), F32),
        )
        results = pl.pallas_call(
            functools.partial(kernel, gx, gy, norm_scale),
            out_shape=shapes,
            in_specs=[far_off] * 7,
            out_specs=(far_off, far_off, far_off),
            scratch_shapes=scratch,
            compiler_params=pltpu.CompilerParams(
                collective_id=0, has_side_effects=True, vmem_limit_bytes=VMEM_BYTES
            ),
            name="evolver",
        )(
            particles,
            neighbours.reshape(16, 16, 16),
            edge_valid.reshape(16, 16, 16),
            dropout_keep.reshape(4, 256, 128),
            weights,
            biases.transpose(1, 0, 2),
            cotangent.reshape(256, 128),
        )
        pgrad, wgrad, bgrad = pl.pallas_call(
            write_out,
            out_shape=shapes,
            in_specs=[far_off] * 3,
            out_specs=(far_off, far_off, far_off),
            scratch_shapes=[vmem(s.shape, s.dtype) for s in shapes]
            + [pltpu.SemaphoreType.DMA((8,)), pltpu.SemaphoreType.DMA((8,))],
            compiler_params=pltpu.CompilerParams(vmem_limit_bytes=VMEM_BYTES),
            name="write_out",
        )(*results)
        return (pgrad.reshape(particles.shape), wgrad, bgrad.transpose(1, 0, 2))

    cells = P("gx", "gy", None, None)
    return jax.shard_map(
        shards,
        mesh=mesh,
        in_specs=(cells, cells, cells, P(None, None, "gx", "gy", None, None), P(), P(), cells),
        out_specs=(cells, P(), P()),
        check_vma=False,
    )
```

time: 72.9 us -> 59.7 us (0.82)
  local copies, waits for them, and re-layouts: 7.53 us -> 0 us
  Pallas kernels: 63.4 us -> 58.9 us
  other arithmetic: 1.02 us -> 0 us
    unnamed x17 -> x0, local copies, waits for them, and re-layouts: 7.52 us -> none
    pallas_call x1 -> x2, Pallas kernels: 63.4 us -> 58.9 us  [the longest x1 56.8 us: shards(): pl.pallas_call(functools.partial(kernel, gx, gy, norm_scale), out_shape=s...]
    mul x2 -> x0, other arithmetic: 1.02 us -> none  [the longest x1 1.02 us: shards(): wgrad.astype(F32) * norm_scale]
where the time goes in v3:
time: 59.7 us; the launch traced here: 59.6 us
  Pallas kernels  58.9 us (99%)
  between operations  0.64 us (1%)
    pallas_call x1, Pallas kernels, shards(): pl.pallas_call(functools.partial(kernel, gx, gy, norm_scale), out_shape=s...  56.8 us
    pallas_call x1, Pallas kernels, shards(): pl.pallas_call(write_out, out_shape=shapes, in_specs=[far_off] * 3, out_s...  2.12 us

profile of v3, /device:TPU:1, one launch (start us, length us, event | category | flops | bytes accessed | tf_op | source)
XLA Modules:
  0.0 59.6 jit_solution(16256616129504893796)
XLA Ops:
  0.6 56.8 %evolver.1 = (f32[256,128]{1,0:T(8,128)}, f32[2,7,128,128]{3,2,1,0:T(8,128)}, f32[3,2,128]{2,1,0:T(2,128)}) custom-call(bf16[4,4,16,128]{3,2,1,0:T(8,128)(2,1)} %part_hbm.1, s32[16,16,16]{2,1,0:T(8,128)} %bitcast.8, s32[16,16,16]{2,1,0:T(8,128)} %bitcast.9, s32[4,256,128]{2,1,0:T(8,128)} %bitcast.7, bf16[2,7,128,128]{3,2,1,0:T(8,128)(2,1)} %w_hbm.1, ...), custom_call_target="tpu_custom_call" | custom-call | tf_op jit(solution)/shard_map/evolver/pallas_call | solution.py:802
  57.5 2.1 %write_out.1 = (f32[256,128]{1,0:T(8,128)}, f32[2,7,128,128]{3,2,1,0:T(8,128)}, f32[3,2,128]{2,1,0:T(2,128)}) custom-call(f32[256,128]{1,0:T(8,128)} %get-tuple-element.9.pgrad, f32[2,7,128,128]{3,2,1,0:T(8,128)} %get-tuple-element.10.wgrad, f32[3,2,128]{2,1,0:T(2,128)} %get-tuple-element.11.bgrad), custom_call_target="tpu_custom_call" | custom-call | tf_op jit(solution)/shard_map/write_out/pallas_call | solution.py:821

commit v4 on v3

--- a/solution.py
+++ b/solution.py
@@ -21,8 +21,9 @@
 TILES = [64, 32, 32]
 BIAS_TILE = 24
 ROUTES = [(1, 0), (-1, 0), (0, 1), (0, -1), (1, 1), (1, -1), (-1, 1), (-1, -1)]
-BORDER = [[0, 1, 2, 3], [12, 13, 14, 15], [4, 8, 7, 11]]
-INSIDE = [[5, 6, 9, 10]]
+BY_X, BY_Y, BY_CORNER = [0, 1], [2, 3], [4, 5, 6, 7]
+SIDE_X, SIDE_Y, CORNERS, INSIDE = [1, 2, 13, 14], [4, 8, 7, 11], [0, 3, 12, 15], [5, 6, 9, 10]
+BORDER = SIDE_X + SIDE_Y + CORNERS
 
 
 def dot(a, b):
@@ -45,10 +46,6 @@
 
 def ones_where(mask):
     return jnp.where(mask, 1.0, 0.0)
-
-
-def flat(fours):
-    return [c for four in fours for c in four]
 
 
 def rows_of(ref, cells):
@@ -118,7 +115,7 @@
     mid_pair,
     *rest,
 ):
-    groups = [rest[n * 6 : n * 6 + 6] for n in range(3)]
+    groups = [rest[0:6], rest[6:12], rest[12:17]]
     (
         in_sem,
         out_sem,
@@ -128,7 +125,7 @@
         back_recv_sem,
         red_send_sem,
         red_recv_sem,
-    ) = rest[18:]
+    ) = rest[17:]
     me_x = lax.axis_index("gx")
     me_y = lax.axis_index("gy")
     depth = gy // Y_HI
@@ -227,6 +224,11 @@
     halos = [halo_copies(layer) for layer in range(2)]
     backs = [back_copies(layer) for layer in range(2)]
 
+    loads[0].wait()
+    pl.semaphore_wait(barrier, plane - 1 + depth - 1 + len(ROUTES))
+    for copy in reversed(halos[0]):
+        copy.start()
+
     spread = ones_where(
         lax.broadcasted_iota(jnp.int32, (16, 256), 1) // 16
         == lax.broadcasted_iota(jnp.int32, (16, 256), 0)
@@ -239,15 +241,10 @@
         lax.broadcasted_iota(jnp.int32, (16, 256), 1) // 16
         == lax.broadcasted_iota(jnp.int32, (16, 256), 0)
     ).astype(BF16)
-    loads[0].wait()
     loads[1].wait()
     loads[2].wait()
     codes = code_ref[...].reshape(256, 16).astype(F32).astype(BF16)
     code_rows[...] = dot(gather_cell, (dot(codes, spread) * own).astype(BF16))
-
-    pl.semaphore_wait(barrier, plane - 1 + depth - 1 + len(ROUTES))
-    for copy in halos[0]:
-        copy.start()
 
     slot_rows = lax.broadcasted_iota(jnp.int32, (144, 256), 0).astype(F32)
     slot_lanes = lax.broadcasted_iota(jnp.int32, (16, 256), 1).astype(F32)
@@ -304,20 +301,21 @@
         far = dot(state, matrix(layer, FAR)).astype(BF16)
         far_tab[1:5, 1:5] = far.reshape(4, 4, 16, 128)
 
-    def halo_projections(layer):
-        for copy in halos[layer]:
-            copy.wait_recv()
-        pieces = [
-            state_tab[layer, 0].reshape(96, 128),
-            state_tab[layer, 5].reshape(96, 128),
-            state_tab[layer, 1:5, 0].reshape(64, 128),
-            state_tab[layer, 1:5, 5].reshape(64, 128),
-        ]
+    def halo_projections(layer, routes):
+        for n in routes:
+            halos[layer][n].wait_recv()
+        places = []
+        for n in routes:
+            dx, dy = ROUTES[n]
+            places.append((part(dx, (0, 5)), part(dy, (0, 5)), 16 if dx and dy else 64))
+        pieces = [state_tab[layer, x, y].reshape(rows, 128) for x, y, rows in places]
         far = dot(jnp.concatenate(pieces, axis=0), matrix(layer, FAR)).astype(BF16)
-        far_tab[0] = far[0:96].reshape(6, 16, 128)
-        far_tab[5] = far[96:192].reshape(6, 16, 128)
-        far_tab[1:5, 0] = far[192:256].reshape(4, 16, 128)
-        far_tab[1:5, 5] = far[256:320].reshape(4, 16, 128)
+        done = 0
+        for n, (x, y, rows) in zip(routes, places):
+            dx, dy = ROUTES[n]
+            shape = (1 if dx else 4, 1 if dy else 4, 16, 128)
+            far_tab[x, y] = far[done : done + rows].reshape(shape)
+            done += rows
 
     def edges_forward(layer, cells):
         fetched = []
@@ -360,34 +358,36 @@
             for n, c in enumerate(cells):
                 state_tab[1, c // 4 + 1, c % 4 + 1] = after[n * 16 : (n + 1) * 16]
 
+    def border_forward(layer):
+        for routes, cells in (
+            (BY_X, SIDE_X),
+            (BY_Y, SIDE_Y),
+            (BY_CORNER, CORNERS),
+        ):
+            halo_projections(layer, routes)
+            edges_forward(layer, cells)
+        nodes_forward(layer, BORDER)
+
     own_projections(0)
-    halo_projections(0)
-    for four in BORDER:
-        edges_forward(0, four)
-    nodes_forward(0, flat(BORDER))
-    for copy in halos[1]:
+    border_forward(0)
+    for copy in reversed(halos[1]):
         copy.start()
-    for four in INSIDE:
-        edges_forward(0, four)
-    nodes_forward(0, flat(INSIDE))
+    edges_forward(0, INSIDE)
+    nodes_forward(0, INSIDE)
     own_projections(1)
-    for four in INSIDE:
-        edges_forward(1, four)
-    nodes_forward(1, flat(INSIDE))
-    halo_projections(1)
-    for four in BORDER:
-        edges_forward(1, four)
-    nodes_forward(1, flat(BORDER))
+    edges_forward(1, INSIDE)
+    nodes_forward(1, INSIDE)
+    border_forward(1)
 
     def node_back(layer, cells):
         up_b = rows_of(upstream, cells).astype(BF16)
-        set_rows(up_b_ref, cells, up_b)
+        set_rows(up_b_ref.at[layer], cells, up_b)
         d_pre = side_dot(up_b, matrix(layer, OUT)) * rows_of(g_node.at[layer], cells)
         d_pre_b = d_pre.astype(BF16)
-        set_rows(d_pre_ref, cells, d_pre_b)
+        set_rows(d_pre_ref.at[layer], cells, d_pre_b)
         keep_msg = kept(layer, 0, cells, keep_scale / 16)
         d_msg = (side_dot(d_pre_b, matrix(layer, MSG)) * keep_msg).astype(BF16)
-        set_rows(d_msg_ref, cells, d_msg)
+        set_rows(d_msg_ref.at[layer], cells, d_msg)
         set_rows(d_pool, cells, side_dot(d_msg, matrix(layer, POOL)).astype(BF16))
         return jnp.sum(d_pre, axis=0, keepdims=True)
 
@@ -402,7 +402,7 @@
         ones = []
         for n, c in enumerate(cells):
             d_one = halves_stacked(outs[n]) * g_one[layer, c].astype(F32)
-            d_near[c * 16 : (c + 1) * 16, :] = jnp.sum(d_one.reshape(16, 16, 128), axis=0)
+            d_near[layer, c * 16 : (c + 1) * 16, :] = jnp.sum(d_one.reshape(16, 16, 128), axis=0)
             ones.append(d_one.astype(BF16))
         both = [
             dot(
@@ -411,48 +411,45 @@
             )
             for n, c in enumerate(cells)
         ]
-        mid_acc[...] += sum(b[:128, :128] for b in both)
+        mid_acc[layer] += sum(b[:128, :128] for b in both)
         for n, c in enumerate(cells):
             x, y = c // 4, c % 4
-            far_acc[x : x + 3, y : y + 3] += both[n][128:, 128:].reshape(3, 3, 16, 128)
+            far_acc[layer, x : x + 3, y : y + 3] += both[n][128:, 128:].reshape(3, 3, 16, 128)
         return mid_b_sum
 
-    def clear_sums():
-        far_acc[...] = jnp.zeros((6, 6, 16, 128), F32)
-        mid_acc[...] = jnp.zeros((128, 128), F32)
-
-    def send_far(layer):
-        far_send[layer, 0] = far_acc[0].astype(BF16)
-        far_send[layer, 5] = far_acc[5].astype(BF16)
-        far_send[layer, 1:5, 0] = far_acc[1:5, 0].astype(BF16)
-        far_send[layer, 1:5, 5] = far_acc[1:5, 5].astype(BF16)
-        for copy in backs[layer]:
-            copy.start()
-
-    def add_arrivals(layer):
-        for n, (dx, dy) in enumerate(ROUTES):
+    def send_far(layer, routes):
+        for n in routes:
+            dx, dy = ROUTES[n]
+            x = pl.ds(1, 4) if dx == 0 else pl.ds(5 if dx > 0 else 0, 1)
+            y = pl.ds(1, 4) if dy == 0 else pl.ds(5 if dy > 0 else 0, 1)
+            far_send[layer, x, y] = far_acc[layer, x, y].astype(BF16)
+            backs[layer][n].start()
+
+    def add_arrivals(layer, routes):
+        for n in routes:
+            dx, dy = ROUTES[n]
             backs[layer][n].wait_recv()
             x = pl.ds(1, 4) if dx == 0 else pl.ds(1 if dx > 0 else 4, 1)
             y = pl.ds(1, 4) if dy == 0 else pl.ds(1 if dy > 0 else 4, 1)
             block = far_recv[layer, n].astype(F32)
             if dx and dy:
-                far_acc[x, y] += block[0:1][None]
+                far_acc[layer, x, y] += block[0:1][None]
             elif dx:
-                far_acc[x, y] += block[None]
+                far_acc[layer, x, y] += block[None]
             else:
-                far_acc[x, y] += block[:, None]
-
-    def far_rows(cells):
+                far_acc[layer, x, y] += block[:, None]
+
+    def far_rows(layer, cells):
         return jnp.concatenate(
-            [far_acc[c // 4 + 1, c % 4 + 1] for c in cells], axis=0
+            [far_acc[layer, c // 4 + 1, c % 4 + 1] for c in cells], axis=0
         ).astype(BF16)
 
     def new_upstream(layer, cells):
         return (
             rows_of(upstream, cells)
-            + side_dot(rows_of(d_pre_ref, cells), matrix(layer, SELF))
-            + side_dot(rows_of(d_near, cells).astype(BF16), matrix(layer, NEAR))
-            + side_dot(far_rows(cells), matrix(layer, FAR))
+            + side_dot(rows_of(d_pre_ref.at[layer], cells), matrix(layer, SELF))
+            + side_dot(rows_of(d_near.at[layer], cells).astype(BF16), matrix(layer, NEAR))
+            + side_dot(far_rows(layer, cells), matrix(layer, FAR))
         )
 
     def spans(n, index):
@@ -475,7 +472,7 @@
                     stage[half, p, offset : offset + count, :] = value[done : done + count]
 
     def take(n):
-        gathered = groups[n][5]
+        gathered = groups[n][-1]
         for index, (layer, m) in enumerate(GROUPS[n]):
             for done, count, half, p, offset in spans(n, index):
                 piece = gathered[half, p, offset : offset + count, :]
@@ -492,22 +489,21 @@
             used += rows - offset
 
     def edge_grads(layer):
-        put(layer, MID, mid_acc[...])
-        near_b = d_near[...].astype(BF16)
+        put(layer, MID, mid_acc[layer])
+        near_b = d_near[layer].astype(BF16)
         put(layer, NEAR, back_dot(inner_state(layer), near_b))
-        far_b = far_acc[...].astype(BF16).reshape(576, 128)
+        far_b = far_acc[layer].astype(BF16).reshape(576, 128)
         put(layer, FAR, back_dot(padded_state(layer), far_b))
-        return jnp.sum(d_near[...], axis=0, keepdims=True)
+        return jnp.sum(d_near[layer], axis=0, keepdims=True)
 
     def node_grads(layer):
-        put(layer, OUT, back_dot(hidden[layer], up_b_ref[...]))
-        put(layer, SELF, back_dot(inner_state(layer), d_pre_ref[...]))
-        put(layer, MSG, back_dot(message[layer], d_pre_ref[...]))
-        put(layer, POOL, back_dot(pooled[layer], d_msg_ref[...]))
-
-    bias_rows = TILES[2] // (2 * plane) * 16
-    bias_chunk, bias_offset = divmod(BIAS_TILE * 16, bias_rows)
-    bias_half, bias_p = divmod(bias_chunk, plane)
+        put(layer, OUT, back_dot(hidden[layer], up_b_ref[layer]))
+        put(layer, SELF, back_dot(inner_state(layer), d_pre_ref[layer]))
+        put(layer, MSG, back_dot(message[layer], d_pre_ref[layer]))
+        put(layer, POOL, back_dot(pooled[layer], d_msg_ref[layer]))
+
+    bias_rows = TILES[2] // plane * 16
+    bias_p, bias_offset = divmod(BIAS_TILE * 16, bias_rows)
     bias_here = slice(bias_offset, bias_offset + 16)
 
     def split_again(tile):
@@ -549,11 +545,6 @@
         core_copy(n).wait_recv()
         total = stage[core].astype(F32) + arrived[...].astype(F32)
         added[...] = total.astype(BF16)
-        if n == 2:
-            tile = total[bias_p, bias_here]
-            added[bias_p, bias_here] = jnp.where(
-                core == bias_half, split_again(tile), tile.astype(BF16)
-            )
 
         def body(d, _):
             p = lax.rem(me_p + d, plane)
@@ -563,14 +554,11 @@
         lax.fori_loop(1, plane, body, 0)
         slots[me_p] = added[me_p]
 
-    def rounded(n, total):
+    def rounded(total):
         plain = total.astype(BF16)
-        if n < 2:
-            return plain
-        mine = jnp.logical_and(core == bias_half, me_p == bias_p)
         pieces = [
             plain[:bias_offset],
-            jnp.where(mine, split_again(total[bias_here]), plain[bias_here]),
+            jnp.where(me_p == bias_p, split_again(total[bias_here]), plain[bias_here]),
             plain[bias_offset + 16 :],
         ]
         return jnp.concatenate([p for p in pieces if p.shape[0]], axis=0)
@@ -578,7 +566,7 @@
     def over_z(n):
         stage, arrived, added, slots, across, gathered = groups[n]
         wait_all(red_recv_sem, 5 * n + 1, slots, plane - 1)
-        across[me_z] = rounded(n, fold(slots, plane))
+        across[me_z] = fold(slots, plane).astype(BF16)
 
         def body(d, _):
             z = lax.rem(me_z + d, depth)
@@ -590,7 +578,7 @@
     def back_over_plane(n):
         stage, arrived, added, slots, across, gathered = groups[n]
         wait_all(red_recv_sem, 5 * n + 2, across, depth - 1)
-        gathered[core, me_p] = rounded(n, fold(across, depth))
+        gathered[core, me_p] = fold(across, depth).astype(BF16)
 
         def body(d, _):
             p = lax.rem(me_p + d, plane)
@@ -609,6 +597,50 @@
         pltpu.make_async_copy(
             groups[n][5].at[1 - core], groups[n][5].at[1 - core], red_recv_sem.at[5 * n + 4]
         ).wait()
+
+    edge_stage, edge_slots, edge_pair, edge_across, edge_gathered = groups[2]
+
+    def edge_core_copy():
+        return remote(edge_pair.at[core], edge_pair.at[core], 11, partner)
+
+    def edge_plane():
+        edge_slots[me_p] = edge_stage[0, me_p]
+
+        def body(d, _):
+            p = lax.rem(me_p + d, plane)
+            remote(edge_stage.at[0, p], edge_slots.at[me_p], 10, plane_device(p)).start()
+            return 0
+
+        lax.fori_loop(1, plane, body, 0)
+
+    def edge_core():
+        wait_all(red_recv_sem, 10, edge_slots, plane - 1)
+        edge_pair[core] = rounded(fold(edge_slots, plane))
+        edge_core_copy().start()
+
+    def edge_z():
+        pltpu.make_async_copy(
+            edge_pair.at[1 - core], edge_pair.at[1 - core], red_recv_sem.at[11]
+        ).wait()
+        edge_across[me_z] = rounded(fold(edge_pair, 2))
+
+        def body(d, _):
+            here = edge_across.at[me_z]
+            remote(here, here, 12, z_device(lax.rem(me_z + d, depth))).start()
+            return 0
+
+        lax.fori_loop(1, depth, body, 0)
+
+    def edge_gather():
+        wait_all(red_recv_sem, 12, edge_across, depth - 1)
+        edge_gathered[0, me_p] = rounded(fold(edge_across, depth))
+
+        def body(d, _):
+            here = edge_gathered.at[0, me_p]
+            remote(here, here, 13, plane_device(lax.rem(me_p + d, plane))).start()
+            return 0
+
+        lax.fori_loop(1, plane, body, 0)
 
     runs = [(1, 0, 7), (0, SELF, 2), (0, POOL, 2), (0, NEAR, 2), (0, MID, 1)]
     outs = [
@@ -625,36 +657,38 @@
     no_sum = jnp.zeros((16, 128), F32)
 
     upstream[...] = cot_ref[...]
-    node_b1 = node_back(1, list(range(16)))
-    clear_sums()
-    mid_b1 = no_sum
-    for four in BORDER:
-        mid_b1 = edges_back(1, four, mid_b1)
-    send_far(1)
-    for four in INSIDE:
-        mid_b1 = edges_back(1, four, mid_b1)
+    for layer in range(2):
+        far_acc[layer] = jnp.zeros((6, 6, 16, 128), F32)
+        mid_acc[layer] = jnp.zeros((128, 128), F32)
+    node_b1 = node_back(1, BORDER + INSIDE)
+    mid_b1 = edges_back(1, CORNERS, no_sum)
+    send_far(1, BY_CORNER)
+    mid_b1 = edges_back(1, SIDE_Y, mid_b1)
+    send_far(1, BY_Y)
+    mid_b1 = edges_back(1, SIDE_X, mid_b1)
+    send_far(1, BY_X)
+    mid_b1 = edges_back(1, INSIDE, mid_b1)
     edge_b1 = edge_grads(1)
     node_grads(1)
     clear_rest(0, len(TOP) * 128)
     over_core(0)
 
-    set_rows(upstream, flat(INSIDE), new_upstream(1, flat(INSIDE)))
-    node_b0 = node_back(0, flat(INSIDE))
+    def start_layer(cells):
+        set_rows(upstream, cells, new_upstream(1, cells))
+        return node_back(0, cells)
+
+    node_b0 = start_layer(INSIDE)
+    mid_b0 = edges_back(0, INSIDE, no_sum)
     over_plane(0)
-    add_arrivals(1)
-    set_rows(upstream, flat(BORDER), new_upstream(1, flat(BORDER)))
-    clear_sums()
-    node_b0 = node_b0 + node_back(0, flat(BORDER))
+    add_arrivals(1, BY_X)
+    node_b0 = node_b0 + start_layer(SIDE_X)
+    mid_b0 = edges_back(0, SIDE_X, mid_b0)
+    add_arrivals(1, BY_Y + BY_CORNER)
+    node_b0 = node_b0 + start_layer(SIDE_Y + CORNERS)
     node_grads(0)
     over_core(1)
-    mid_b0 = no_sum
-    for four in BORDER:
-        mid_b0 = edges_back(0, four, mid_b0)
-    send_far(0)
-    over_plane(1)
-    over_z(0)
-    for four in INSIDE:
-        mid_b0 = edges_back(0, four, mid_b0)
+    mid_b0 = edges_back(0, CORNERS, mid_b0)
+    mid_b0 = edges_back(0, SIDE_Y, mid_b0)
     edge_b0 = edge_grads(0)
     column = [jnp.sum(v, axis=0, keepdims=True) for v in (mid_b0, mid_b1)]
     sums = jnp.concatenate(
@@ -662,21 +696,22 @@
         axis=0,
     )
     high = sums.astype(BF16).astype(F32)
-    groups[2][0][bias_half, bias_p, bias_here, :] = jnp.concatenate(
-        [high, sums - high], axis=0
-    ).astype(BF16)
+    edge_stage[0, bias_p, bias_here, :] = jnp.concatenate([high, sums - high], axis=0).astype(BF16)
     clear_rest(2, (BIAS_TILE + 1) * 16)
-    over_core(2)
+    edge_plane()
+    send_far(0, BY_CORNER + BY_Y + BY_X)
+    over_plane(1)
+    over_z(0)
+    edge_core()
     back_over_plane(0)
-    over_plane(2)
-    over_z(1)
-    add_arrivals(0)
+    edge_z()
+    add_arrivals(0, BY_X + BY_Y + BY_CORNER)
     pgrad_ref[...] = new_upstream(0, list(range(16)))
     outs[5].start()
-    over_z(2)
+    over_z(1)
+    edge_gather()
+    back_over_core(0)
     back_over_plane(1)
-    back_over_core(0)
-    back_over_plane(2)
     arrived_whole(0)
     take(0)
     outs[0].start()
@@ -685,12 +720,11 @@
     take(1)
     outs[1].start()
     outs[2].start()
-    back_over_core(2)
-    arrived_whole(2)
+    wait_all(red_recv_sem, 13, edge_gathered.at[0], plane - 1)
     take(2)
     outs[3].start()
     outs[4].start()
-    pair = groups[2][5][bias_half, bias_p, bias_here, :].astype(F32)
+    pair = edge_gathered[0, bias_p, bias_here, :].astype(F32)
     bias_total = (pair[0:8] + pair[8:16]) * norm_scale
     for m in range(3):
         bgrad_ref[m] = bias_total[2 * m : 2 * m + 2]
@@ -699,13 +733,17 @@
     for layer in range(2):
         for copy in halos[layer] + backs[layer]:
             copy.wait_send()
-    for n in range(3):
+    for n in range(2):
         stage, arrived, added, slots, across, gathered = groups[n]
         core_copy(n).wait_send()
         wait_all(red_send_sem, 5 * n + 1, slots, plane - 1)
         wait_all(red_send_sem, 5 * n + 2, across, depth - 1)
         wait_all(red_send_sem, 5 * n + 3, gathered.at[core], plane - 1)
         share_copy(n).wait_send()
+    wait_all(red_send_sem, 10, edge_slots, plane - 1)
+    edge_core_copy().wait_send()
+    wait_all(red_send_sem, 12, edge_across, depth - 1)
+    wait_all(red_send_sem, 13, edge_gathered.at[0], plane - 1)
     for out in outs:
         out.wait()
 
@@ -769,20 +807,28 @@
             vmem((2, 256, 128), BF16),
             vmem((2, 256, 128), BF16),
             vmem((2, 256, 128), F32),
+            vmem((2, 256, 128), BF16),
+            vmem((256, 128), F32),
+            vmem((2, 256, 128), BF16),
+            vmem((2, 256, 128), BF16),
             vmem((256, 128), BF16),
-            vmem((256, 128), F32),
-            vmem((256, 128), BF16),
-            vmem((256, 128), BF16),
-            vmem((256, 128), BF16),
-            vmem((256, 128), F32),
-            vmem((6, 6, 16, 128), F32),
+            vmem((2, 256, 128), F32),
+            vmem((2, 6, 6, 16, 128), F32),
             vmem((2, 6, 6, 16, 128), BF16),
             vmem((2, 8, 4, 16, 128), BF16),
-            vmem((128, 128), F32),
+            vmem((2, 128, 128), F32),
             vmem((2, 256, 256), BF16),
         ]
-        for tiles in TILES:
+        for tiles in TILES[:2]:
             scratch += group_buffers(tiles)
+        rows = TILES[2] // plane * 16
+        scratch += [
+            vmem((1, plane, rows, 128), BF16),
+            vmem((plane, rows, 128), BF16),
+            vmem((2, rows, 128), BF16),
+            vmem((depth, rows, 128), BF16),
+            vmem((1, plane, rows, 128), BF16),
+        ]
         scratch += [
             pltpu.SemaphoreType.DMA((7,)),
             pltpu.SemaphoreType.DMA((7,)),

time: 59.7 us -> 55.6 us (0.931)
  Pallas kernels: 58.9 us -> 54.9 us
    pallas_call x1, Pallas kernels: 56.8 us -> 52.7 us  [shards(): pl.pallas_call(functools.partial(kernel, gx, gy, norm_scale), out_shape=s...]
where the time goes in v4:
time: 55.6 us; the launch traced here: 55.5 us
  Pallas kernels  54.9 us (99%)
  between operations  0.64 us (1%)
    pallas_call x1, Pallas kernels, shards(): pl.pallas_call(functools.partial(kernel, gx, gy, norm_scale), out_shape=s...  52.7 us
    pallas_call x1, Pallas kernels, shards(): pl.pallas_call(write_out, out_shape=shapes, in_specs=[far_off] * 3, out_s...  2.12 us

profile of v4, /device:TPU:1, one launch (start us, length us, event | category | flops | bytes accessed | tf_op | source)
XLA Modules:
  0.0 55.5 jit_solution(5456346731581174947)
XLA Ops:
  0.6 52.7 %evolver.1 = (f32[256,128]{1,0:T(8,128)}, f32[2,7,128,128]{3,2,1,0:T(8,128)}, f32[3,2,128]{2,1,0:T(2,128)}) custom-call(bf16[4,4,16,128]{3,2,1,0:T(8,128)(2,1)} %part_hbm.1, s32[16,16,16]{2,1,0:T(8,128)} %bitcast.8, s32[16,16,16]{2,1,0:T(8,128)} %bitcast.9, s32[4,256,128]{2,1,0:T(8,128)} %bitcast.7, bf16[2,7,128,128]{3,2,1,0:T(8,128)(2,1)} %w_hbm.1, ...), custom_call_target="tpu_custom_call" | custom-call | tf_op jit(solution)/shard_map/evolver/pallas_call | solution.py:848
  53.4 2.1 %write_out.1 = (f32[256,128]{1,0:T(8,128)}, f32[2,7,128,128]{3,2,1,0:T(8,128)}, f32[3,2,128]{2,1,0:T(2,128)}) custom-call(f32[256,128]{1,0:T(8,128)} %get-tuple-element.9.pgrad, f32[2,7,128,128]{3,2,1,0:T(8,128)} %get-tuple-element.10.wgrad, f32[3,2,128]{2,1,0:T(2,128)} %get-tuple-element.11.bgrad), custom_call_target="tpu_custom_call" | custom-call | tf_op jit(solution)/shard_map/write_out/pallas_call | solution.py:867

commit v5 on v4

--- a/solution.py
+++ b/solution.py
@@ -688,6 +688,7 @@
     node_grads(0)
     over_core(1)
     mid_b0 = edges_back(0, CORNERS, mid_b0)
+    over_plane(1)
     mid_b0 = edges_back(0, SIDE_Y, mid_b0)
     edge_b0 = edge_grads(0)
     column = [jnp.sum(v, axis=0, keepdims=True) for v in (mid_b0, mid_b1)]
@@ -699,19 +700,18 @@
     edge_stage[0, bias_p, bias_here, :] = jnp.concatenate([high, sums - high], axis=0).astype(BF16)
     clear_rest(2, (BIAS_TILE + 1) * 16)
     edge_plane()
+    over_z(0)
     send_far(0, BY_CORNER + BY_Y + BY_X)
-    over_plane(1)
-    over_z(0)
+    over_z(1)
     edge_core()
     back_over_plane(0)
     edge_z()
     add_arrivals(0, BY_X + BY_Y + BY_CORNER)
     pgrad_ref[...] = new_upstream(0, list(range(16)))
     outs[5].start()
-    over_z(1)
+    back_over_plane(1)
     edge_gather()
     back_over_core(0)
-    back_over_plane(1)
     arrived_whole(0)
     take(0)
     outs[0].start()

time: 55.6 us -> 52.4 us (0.942)
  Pallas kernels: 54.9 us -> 51.5 us
    pallas_call x1, Pallas kernels: 52.7 us -> 49.4 us  [shards(): pl.pallas_call(functools.partial(kernel, gx, gy, norm_scale), out_shape=s...]
where the time goes in v5:
time: 52.4 us; the launch traced here: 52.2 us
  Pallas kernels  51.5 us (98%)
  between operations  0.64 us (1%)
    pallas_call x1, Pallas kernels, shards(): pl.pallas_call(functools.partial(kernel, gx, gy, norm_scale), out_shape=s...  49.4 us
    pallas_call x1, Pallas kernels, shards(): pl.pallas_call(write_out, out_shape=shapes, in_specs=[far_off] * 3, out_s...  2.12 us

profile of v5, /device:TPU:1, one launch (start us, length us, event | category | flops | bytes accessed | tf_op | source)
XLA Modules:
  0.0 52.2 jit_solution(7260784453903224775)
XLA Ops:
  0.6 49.4 %evolver.1 = (f32[256,128]{1,0:T(8,128)}, f32[2,7,128,128]{3,2,1,0:T(8,128)}, f32[3,2,128]{2,1,0:T(2,128)}) custom-call(bf16[4,4,16,128]{3,2,1,0:T(8,128)(2,1)} %part_hbm.1, s32[16,16,16]{2,1,0:T(8,128)} %bitcast.8, s32[16,16,16]{2,1,0:T(8,128)} %bitcast.9, s32[4,256,128]{2,1,0:T(8,128)} %bitcast.7, bf16[2,7,128,128]{3,2,1,0:T(8,128)(2,1)} %w_hbm.1, ...), custom_call_target="tpu_custom_call" | custom-call | tf_op jit(solution)/shard_map/evolver/pallas_call | solution.py:848
  50.0 2.1 %write_out.1 = (f32[256,128]{1,0:T(8,128)}, f32[2,7,128,128]{3,2,1,0:T(8,128)}, f32[3,2,128]{2,1,0:T(2,128)}) custom-call(f32[256,128]{1,0:T(8,128)} %get-tuple-element.9.pgrad, f32[2,7,128,128]{3,2,1,0:T(8,128)} %get-tuple-element.10.wgrad, f32[3,2,128]{2,1,0:T(2,128)} %get-tuple-element.11.bgrad), custom_call_target="tpu_custom_call" | custom-call | tf_op jit(solution)/shard_map/write_out/pallas_call | solution.py:867

commit v6 on v5

--- a/solution.py
+++ b/solution.py
@@ -369,6 +369,10 @@
         nodes_forward(layer, BORDER)
 
     own_projections(0)
+    upstream[...] = cot_ref[...]
+    for layer in range(2):
+        far_acc[layer] = jnp.zeros((6, 6, 16, 128), F32)
+        mid_acc[layer] = jnp.zeros((128, 128), F32)
     border_forward(0)
     for copy in reversed(halos[1]):
         copy.start()
@@ -476,7 +480,7 @@
         for index, (layer, m) in enumerate(GROUPS[n]):
             for done, count, half, p, offset in spans(n, index):
                 piece = gathered[half, p, offset : offset + count, :]
-                wgrad_ref[layer, m, done : done + count, :] = piece.astype(F32) * norm_scale
+                wgrad_ref[layer, m, done : done + count, :] = piece
 
     def clear_rest(n, used):
         stage = groups[n][0]
@@ -656,10 +660,6 @@
 
     no_sum = jnp.zeros((16, 128), F32)
 
-    upstream[...] = cot_ref[...]
-    for layer in range(2):
-        far_acc[layer] = jnp.zeros((6, 6, 16, 128), F32)
-        mid_acc[layer] = jnp.zeros((128, 128), F32)
     node_b1 = node_back(1, BORDER + INSIDE)
     mid_b1 = edges_back(1, CORNERS, no_sum)
     send_far(1, BY_CORNER)
@@ -688,8 +688,8 @@
     node_grads(0)
     over_core(1)
     mid_b0 = edges_back(0, CORNERS, mid_b0)
+    mid_b0 = edges_back(0, SIDE_Y, mid_b0)
     over_plane(1)
-    mid_b0 = edges_back(0, SIDE_Y, mid_b0)
     edge_b0 = edge_grads(0)
     column = [jnp.sum(v, axis=0, keepdims=True) for v in (mid_b0, mid_b1)]
     sums = jnp.concatenate(
@@ -748,19 +748,43 @@
         out.wait()
 
 
-def write_out(pgrad, wgrad, bgrad, pgrad_out, wgrad_out, bgrad_out, pbuf, wbuf, bbuf, in_sems, out_sems):
-    routes = [(pgrad, pbuf, pgrad_out), (bgrad, bbuf, bgrad_out)]
-    for layer in range(2):
-        for m, count in ((0, 2), (2, 2), (4, 3)):
-            part = (layer, pl.ds(m, count))
-            routes.append((wgrad.at[part], wbuf.at[part], wgrad_out.at[part]))
-    reads = [pltpu.make_async_copy(a, b, in_sems.at[n]) for n, (a, b, _) in enumerate(routes)]
-    writes = [pltpu.make_async_copy(b, c, out_sems.at[n]) for n, (_, b, c) in enumerate(routes)]
+def write_out(
+    norm_scale,
+    pgrad,
+    wgrad,
+    bgrad,
+    pgrad_out,
+    wgrad_out,
+    bgrad_out,
+    pbuf,
+    wbuf,
+    bbuf,
+    narrow,
+    in_sems,
+    out_sems,
+):
+    parts = [(layer, pl.ds(m, count)) for layer in range(2) for m, count in ((0, 2), (2, 2), (4, 3))]
+    reads = [
+        pltpu.make_async_copy(wgrad.at[part], narrow.at[part], in_sems.at[n])
+        for n, part in enumerate(parts)
+    ]
+    reads.append(pltpu.make_async_copy(pgrad, pbuf, in_sems.at[6]))
+    reads.append(pltpu.make_async_copy(bgrad, bbuf, in_sems.at[7]))
+    writes = [
+        pltpu.make_async_copy(wbuf.at[part], wgrad_out.at[part], out_sems.at[n])
+        for n, part in enumerate(parts)
+    ]
+    writes.append(pltpu.make_async_copy(pbuf, pgrad_out, out_sems.at[6]))
+    writes.append(pltpu.make_async_copy(bbuf, bgrad_out, out_sems.at[7]))
     for read in reads:
         read.start()
-    for read, write in zip(reads, writes):
-        read.wait()
-        write.start()
+    for n, part in enumerate(parts):
+        reads[n].wait()
+        wbuf[part] = narrow[part].astype(F32) * norm_scale
+        writes[n].start()
+    for n in (6, 7):
+        reads[n].wait()
+        writes[n].start()
     for write in writes:
         write.wait()
 
@@ -785,7 +809,7 @@
     def shards(particles, neighbours, edge_valid, dropout_keep, weights, biases, cotangent):
         scratch = [
             vmem((256, 128), F32),
-            vmem((2, 7, 128, 128), F32),
+            vmem((2, 7, 128, 128), BF16),
             vmem((3, 2, 128), F32),
             vmem((16, 16, 16), jnp.int32),
             vmem((16, 16, 16), jnp.int32),
@@ -847,7 +871,7 @@
         )
         results = pl.pallas_call(
             functools.partial(kernel, gx, gy, norm_scale),
-            out_shape=shapes,
+            out_shape=(shapes[0], jax.ShapeDtypeStruct((2, 7, 128, 128), BF16), shapes[2]),
             in_specs=[far_off] * 7,
             out_specs=(far_off, far_off, far_off),
             scratch_shapes=scratch,
@@ -865,11 +889,12 @@
             cotangent.reshape(256, 128),
         )
         pgrad, wgrad, bgrad = pl.pallas_call(
-            write_out,
+            functools.partial(write_out, norm_scale),
             out_shape=shapes,
             in_specs=[far_off] * 3,
             out_specs=(far_off, far_off, far_off),
             scratch_shapes=[vmem(s.shape, s.dtype) for s in shapes]
+            + [vmem((2, 7, 128, 128), BF16)]
             + [pltpu.SemaphoreType.DMA((8,)), pltpu.SemaphoreType.DMA((8,))],
             compiler_params=pltpu.CompilerParams(vmem_limit_bytes=VMEM_BYTES),
             name="write_out",

time: 52.4 us -> 52.1 us (level)
  no operation moved by 1% of the time
where the time goes in v6:
time: 52.1 us; the launch traced here: 52 us
  Pallas kernels  51.3 us (98%)
  between operations  0.64 us (1%)
    pallas_call x1, Pallas kernels, shards(): pl.pallas_call(functools.partial(kernel, gx, gy, norm_scale), out_shape=(...  49.3 us
    pallas_call x1, Pallas kernels, shards(): pl.pallas_call(functools.partial(write_out, norm_scale), out_shape=shapes...  1.99 us

profile of v6, /device:TPU:1, one launch (start us, length us, event | category | flops | bytes accessed | tf_op | source)
XLA Modules:
  0.0 52.0 jit_solution(13314308172444123039)
XLA Ops:
  0.6 49.3 %evolver.1 = (f32[256,128]{1,0:T(8,128)}, bf16[2,7,128,128]{3,2,1,0:T(8,128)(2,1)}, f32[3,2,128]{2,1,0:T(2,128)}) custom-call(bf16[4,4,16,128]{3,2,1,0:T(8,128)(2,1)} %part_hbm.1, s32[16,16,16]{2,1,0:T(8,128)} %bitcast.8, s32[16,16,16]{2,1,0:T(8,128)} %bitcast.9, s32[4,256,128]{2,1,0:T(8,128)} %bitcast.7, bf16[2,7,128,128]{3,2,1,0:T(8,128)(2,1)} %w_hbm.1, ...), custom_call_target="tpu_custom_call" | custom-call | tf_op jit(solution)/shard_map/evolver/pallas_call | solution.py:872
  50.0 2.0 %write_out.1 = (f32[256,128]{1,0:T(8,128)}, f32[2,7,128,128]{3,2,1,0:T(8,128)}, f32[3,2,128]{2,1,0:T(2,128)}) custom-call(f32[256,128]{1,0:T(8,128)} %get-tuple-element.9.pgrad, bf16[2,7,128,128]{3,2,1,0:T(8,128)(2,1)} %get-tuple-element.10.wgrad, f32[3,2,128]{2,1,0:T(2,128)} %get-tuple-element.11.bgrad), custom_call_target="tpu_custom_call" | custom-call | tf_op jit(solution)/shard_map/write_out/pallas_call | solution.py:891

commit v7 on v6

--- a/solution.py
+++ b/solution.py
@@ -706,10 +706,10 @@
     edge_core()
     back_over_plane(0)
     edge_z()
+    back_over_plane(1)
     add_arrivals(0, BY_X + BY_Y + BY_CORNER)
     pgrad_ref[...] = new_upstream(0, list(range(16)))
     outs[5].start()
-    back_over_plane(1)
     edge_gather()
     back_over_core(0)
     arrived_whole(0)

time: 52.1 us -> 52 us (level)
  no operation moved by 1% of the time
where the time goes in v7:
time: 52 us; the launch traced here: 51.9 us
  Pallas kernels  51.3 us (99%)
  between operations  0.64 us (1%)
    pallas_call x1, Pallas kernels, shards(): pl.pallas_call(functools.partial(kernel, gx, gy, norm_scale), out_shape=(...  49.3 us
    pallas_call x1, Pallas kernels, shards(): pl.pallas_call(functools.partial(write_out, norm_scale), out_shape=shapes...  1.99 us

profile of v7, /device:TPU:1, one launch (start us, length us, event | category | flops | bytes accessed | tf_op | source)
XLA Modules:
  0.0 51.9 jit_solution(16114091500719122315)
XLA Ops:
  0.6 49.3 %evolver.1 = (f32[256,128]{1,0:T(8,128)}, bf16[2,7,128,128]{3,2,1,0:T(8,128)(2,1)}, f32[3,2,128]{2,1,0:T(2,128)}) custom-call(bf16[4,4,16,128]{3,2,1,0:T(8,128)(2,1)} %part_hbm.1, s32[16,16,16]{2,1,0:T(8,128)} %bitcast.8, s32[16,16,16]{2,1,0:T(8,128)} %bitcast.9, s32[4,256,128]{2,1,0:T(8,128)} %bitcast.7, bf16[2,7,128,128]{3,2,1,0:T(8,128)(2,1)} %w_hbm.1, ...), custom_call_target="tpu_custom_call" | custom-call | tf_op jit(solution)/shard_map/evolver/pallas_call | solution.py:872
  49.9 2.0 %write_out.1 = (f32[256,128]{1,0:T(8,128)}, f32[2,7,128,128]{3,2,1,0:T(8,128)}, f32[3,2,128]{2,1,0:T(2,128)}) custom-call(f32[256,128]{1,0:T(8,128)} %get-tuple-element.9.pgrad, bf16[2,7,128,128]{3,2,1,0:T(8,128)(2,1)} %get-tuple-element.10.wgrad, f32[3,2,128]{2,1,0:T(2,128)} %get-tuple-element.11.bgrad), custom_call_target="tpu_custom_call" | custom-call | tf_op jit(solution)/shard_map/write_out/pallas_call | solution.py:891
